TPU v7x, 512 devices: a whole 4x8x8 slice. The times are simulated.
512 devices in a mesh: grp: 8 (over x, core), seq: 64 (over z, y).
Axes of the slice: x: 4, y: 8, z: 8, core: 2. Of those that a mesh axis runs over, the one named last changes fastest.
Arguments:
- llm_grad: bfloat16 [16384, 8192], P('seq', 'grp'), may hold values from -6 to 6
- image_grid: int32 [4096, 2], replicated, may hold values from 1 to 3, as said below
- image_owner: int32 [4096], replicated, may hold values from 0 to 63, as said below
- row_start: int32 [4096], replicated, may hold values from 0 to 255, as said below
- merger_pre: bfloat16 [192, 64, 2560], P(None, 'seq', 'grp'), may hold values from -6 to 6
- vit_out: bfloat16 [768, 64, 1280], P(None, 'seq'), may hold values from -6 to 6
- vit_pre: bfloat16 [768, 64, 2560], P(None, 'seq', 'grp'), may hold values from -6 to 6
- ln_gain: float32 [1280], replicated, may hold values from 0.25 to 1.75
- merger_out_w: bfloat16 [8192, 2560], P('seq', 'grp'), may hold values from -0.0625 to 0.0625
- merger_in_w: bfloat16 [2560, 5120], P('grp', 'seq'), may hold values from -0.125 to 0.125
- vit_fc2_w: bfloat16 [1280, 2560], P('seq', 'grp'), may hold values from -0.15625 to 0.15625
Outputs:
- patch_grad: bfloat16 [768, 64, 1280], P('grp', 'seq')
- fc1_grad: bfloat16 [768, 64, 2560], P(None, 'seq', 'grp')
- fc2_w_grad: float32 [1280, 2560], P('seq', 'grp')
Inputs may be any that keep to these rules, and one draw needn't show every extreme that they name: `image_grid`: height times width is 1 to 3; the first image of every shard is 1 by 3; the last image of shard 0 is 1 by 1. `image_owner`: the 64 images of one shard have 64 different owners. An image's rows row_start to row_start + t - 1 lie inside its shard and meet no other image's rows; a shard's images follow the order of k; the last image of every shard ends at the shard's last row; the first image of shard 0 starts at row 0.
All inputs are finite; a program needn't handle non-finite values.
Results may differ from a plain program's by a relative error of at most 0.02.
Values may be sent and summed in bfloat16 or wider, within the bound.
No kernel may reach another device: no remote copies, remote signals or barrier semaphores. Data moves between devices by JAX's collectives and lax.ppermute only.
A program may use at most 64 MiB of HBM per device.

v0:
```python
import jax
import jax.numpy as jnp
from jax import lax
from jax.sharding import Mesh
from jax.sharding import PartitionSpec as P

SLOT = 3
SEQ = ("seq_0", "seq_1")


def joined_along(tiles, dim):
    tiles = jnp.moveaxis(tiles, 0, dim)
    lengths = tiles.shape
    return tiles.reshape(*lengths[:dim], lengths[dim] * lengths[dim + 1], *lengths[dim + 2 :])


def gather_in_order(value, axes, order):
    tiles = value[None]
    for k in order:
        tiles = lax.all_gather(tiles, axes[k], axis=0, tiled=True)
    current = [lax.axis_size(axes[k]) for k in reversed(order)]
    tiles = tiles.reshape(*current, *value.shape)
    turned = sorted(range(len(order)), key=lambda place: order[len(order) - 1 - place])
    return tiles.transpose(*turned, *range(len(order), tiles.ndim)).reshape(-1, *value.shape)


def gather_axes(value, axes, order, dim):
    return joined_along(gather_in_order(value, axes, order), dim)


def filled_up(lines, size):
    spare = -lines.shape[0] % size
    if not spare:
        return lines
    return jnp.concatenate([lines, jnp.zeros((spare, *lines.shape[1:]), lines.dtype)])


def sum_by_parts(value, axis):
    lines = value.reshape(-1, *value.shape[1:][-1:])
    own = lax.psum_scatter(
        filled_up(lines, lax.axis_size(axis)), axis, scatter_dimension=0, tiled=True
    )
    whole = lax.all_gather(own, axis).reshape(-1, *lines.shape[1:])
    return lax.slice_in_dim(whole, 0, len(lines)).reshape(value.shape)


def copy_for_each(value, axis):
    copies = jnp.broadcast_to(value, (lax.axis_size(axis), *value.shape))
    return lax.all_to_all(copies, axis, split_axis=0, concat_axis=0, tiled=True)


def gather_directly(value, axis, dim):
    return joined_along(copy_for_each(value, axis), dim)


def in_blocks(value, dim, size):
    lengths = value.shape
    tiles = value.reshape(*lengths[:dim], size, lengths[dim] // size, *lengths[dim + 1 :])
    return jnp.moveaxis(tiles, dim, 0)


def sum_at_owner(value, axis, dim):
    tiles = in_blocks(value, dim, lax.axis_size(axis))
    arrived = lax.all_to_all(tiles, axis, split_axis=0, concat_axis=0, tiled=True)
    return arrived.astype(jnp.float32).sum(axis=0)


def gelu_slope(values):
    return (
        0.5 * (1.0 + lax.erf(values * 0.7071067811865476))
        + values * jnp.exp(-0.5 * values * values) * 0.3989422804014327
    )


def patch_table(widths, counts, slots):
    places = jnp.arange(4 * slots, dtype=jnp.int32)
    merged = places // 4
    corner = places % 4
    row_in = merged[None, :] // widths[:, None]
    col_in = merged[None, :] % widths[:, None]
    target = (
        (2 * row_in + corner[None, :] // 2) * (2 * widths[:, None])
        + 2 * col_in
        + corner[None, :] % 2
    )
    usable = merged[None, :] < counts[:, None]
    return ((target[:, None, :] == places[None, :, None]) & usable[:, None, :]).astype(jnp.float32)


def norm_backward(upstream, inputs, scales):
    average = jnp.mean(inputs, -1, keepdims=True)
    centred = inputs - average
    inverse_std = lax.rsqrt(jnp.mean(centred * centred, -1, keepdims=True) + 1e-06)
    normed = centred * inverse_std
    scaled = upstream * scales
    return inverse_std * (
        scaled
        - jnp.mean(scaled, -1, keepdims=True)
        - normed * jnp.mean(scaled * normed, -1, keepdims=True)
    )


def on_device(
    llm_grad,
    image_grid,
    image_owner,
    row_start,
    merger_pre,
    vit_out,
    vit_pre,
    ln_gain,
    merger_out_w,
    merger_in_w,
    vit_fc2_w,
):
    seq_count = lax.axis_size(SEQ)
    own_index = lax.axis_index(SEQ)
    grids = image_grid.reshape(seq_count, seq_count, 2)
    counts = grids[:, :, 0] * grids[:, :, 1]
    widths = grids[:, :, 1]
    owners = image_owner.reshape(seq_count, seq_count)
    starts = row_start.reshape(seq_count, seq_count)
    within = jnp.arange(SLOT, dtype=jnp.int32)
    peers = jnp.arange(seq_count, dtype=jnp.int32)
    shard_rows = llm_grad.shape[0]
    my_owners = lax.dynamic_index_in_dim(owners, own_index, 0, keepdims=False)
    my_counts = lax.dynamic_index_in_dim(counts, own_index, 0, keepdims=False)
    my_starts = lax.dynamic_index_in_dim(starts, own_index, 0, keepdims=False)
    targets = (my_owners[None, :] == peers[:, None]).astype(jnp.int32)
    send_counts = jnp.sum(targets * my_counts[None, :], 1)
    send_starts = jnp.sum(targets * my_starts[None, :], 1)
    indices = jnp.minimum(send_starts[:, None] + within[None, :], shard_rows - 1)
    usable = within[None, :] < send_counts[:, None]
    picked = jnp.take(llm_grad, indices.reshape(-1), axis=0)
    outgoing = jnp.where(usable.reshape(-1, 1), picked, jnp.zeros_like(picked)).reshape(
        seq_count, SLOT, llm_grad.shape[1]
    )
    received = (owners == own_index).astype(jnp.int32)
    recv_counts = jnp.sum(received * counts, 1)
    recv_widths = jnp.sum(received * widths, 1)
    wide_rows = lax.all_gather(outgoing, "grp", axis=2, tiled=True)
    flat = wide_rows.reshape(-1, wide_rows.shape[2])
    columns = flat
    folded = jnp.dot(
        columns, gather_axes(merger_out_w, SEQ, (0, 1), 0), preferred_element_type=jnp.float32
    )
    source_grad = folded.astype(jnp.bfloat16).reshape(seq_count, SLOT, merger_out_w.shape[1])
    arrived = lax.all_to_all(source_grad, SEQ, split_axis=0, concat_axis=0, tiled=True)
    unit_grad = arrived.reshape(seq_count * SLOT, merger_out_w.shape[1])
    pre_act = merger_pre[:, 0, :].astype(jnp.float32)
    pre_grad = (gelu_slope(pre_act) * unit_grad.astype(jnp.float32)).astype(jnp.bfloat16)
    merged_part = jnp.dot(
        pre_grad,
        lax.all_gather(merger_in_w, SEQ, axis=1, tiled=True),
        preferred_element_type=jnp.float32,
    )
    vit_width = vit_out.shape[2]
    table = patch_table(recv_widths, recv_counts, SLOT)
    patch_part = jnp.einsum(
        "spq,sqc->spc",
        table,
        merged_part.reshape(seq_count, 4 * SLOT, vit_width),
        precision=lax.Precision.HIGHEST,
    ).reshape(-1, vit_width)
    patch_in = sum_by_parts(patch_part.astype(jnp.bfloat16), "grp").astype(jnp.float32)
    patch_grad = norm_backward(patch_in, vit_out[:, 0, :].astype(jnp.float32), ln_gain).astype(
        jnp.bfloat16
    )
    group_rows = patch_grad.shape[0] // lax.axis_size("grp")
    own_rows = lax.dynamic_slice_in_dim(
        patch_grad, lax.axis_index("grp") * group_rows, group_rows, 0
    )
    columns = patch_grad
    act_grad = jnp.dot(
        columns, gather_directly(vit_fc2_w, SEQ, 0), preferred_element_type=jnp.float32
    )
    fc_in = vit_pre[:, 0, :].astype(jnp.float32)
    sigmoid_q = jax.nn.sigmoid(1.702 * fc_in)
    activation = (fc_in * sigmoid_q).astype(jnp.bfloat16)
    fc1_grad = ((sigmoid_q + 1.702 * fc_in * sigmoid_q * (1.0 - sigmoid_q)) * act_grad).astype(
        jnp.bfloat16
    )
    columns = patch_grad
    weight_grad = sum_at_owner(
        lax.dot_general(
            columns, activation, (((0,), (0,)), ((), ())), preferred_element_type=jnp.float32
        ).astype(jnp.bfloat16),
        SEQ,
        0,
    )
    return (
        own_rows.reshape(group_rows, 1, vit_width),
        fc1_grad.reshape(-1, 1, vit_pre.shape[2]),
        weight_grad,
    )


def solution(mesh):
    finer = Mesh(mesh.devices.reshape(mesh.shape["grp"], 8, 8), ("grp", "seq_0", "seq_1"))
    in_specs = (
        P(SEQ, "grp"),
        P(),
        P(),
        P(),
        P(None, SEQ, "grp"),
        P(None, SEQ, None),
        P(None, SEQ, "grp"),
        P(),
        P(SEQ, "grp"),
        P("grp", SEQ),
        P(SEQ, "grp"),
    )
    out_specs = (P("grp", SEQ, None), P(None, SEQ, "grp"), P(SEQ, "grp"))
    return jax.shard_map(
        on_device, mesh=finer, in_specs=in_specs, out_specs=out_specs, check_vma=False
    )
```

profile of v0, /device:TPU:8, one launch (start us, length us, event | category | flops | bytes accessed | tf_op | source)
XLA Modules:
  0.0 368.1 jit_solution(14716126669979269962)
XLA Ops:
  13.1 30.2 %all-gather = bf16[1024,320]{0,1:T(8,128)(2,1)S(1)} all-gather(bf16[128,320]{0,1:T(8,128)(2,1)S(1)} %copy-done.7), channel_id=2, replica_groups=mesh['grp'=8,'seq_0'=8,'seq_1'=8] {'seq_0'}, dimensions={0}, use_global_device_ids=true | all-gather | bytes 737280 | tf_op jit(solution)/shard_map/all_gather | solution.py:20
  45.1 10.1 %all-gather.7.cloned.1.call-done = bf16[64,3,8192]{2,1,0:T(4,128)(2,1)} async-done(((bf16[64,3,1024]{2,1,0:T(4,128)(2,1)}), bf16[64,3,8192]{2,1,0:T(4,128)(2,1)}) %all-gather.7.cloned.1.call-update) | async-done | bytes 3145744 | tf_op jit(solution)/shard_map/all_gather | solution.py:141
  55.2 7.4 %reshape.530 = bf16[192,8192]{1,0:T(8,128)(2,1)} reshape(bf16[64,3,8192]{2,1,0:T(4,128)(2,1)} %all-gather.7.cloned.1.call-done) | data formatting | bytes 6291456 | tf_op jit(solution)/shard_map/reshape | solution.py:142
  62.6 68.7 %all-gather.9.cloned.1.call-done = bf16[64,128,320]{1,0,2:T(8,128)(2,1)} async-done(((bf16[8,128,320]{1,0,2:T(8,128)(2,1)}), bf16[64,128,320]{1,0,2:T(8,128)(2,1)}) %all-gather.9.cloned.1.call-update) | async-done | bytes 5242896 | tf_op jit(solution)/shard_map/all_gather | solution.py:20
  131.4 4.0 %copy.25 = bf16[8,8,128,320]{2,1,0,3:T(8,128)(2,1)S(1)} copy(bf16[8,8,128,320]{2,0,1,3:T(8,128)(2,1)} %bitcast.87) | data formatting | bytes 10485760 | tf_op jit(solution)/shard_map/transpose | solution.py:24
  135.4 4.3 %fusion.9 = bf16[192,320]{1,0:T(8,128)(2,1)S(1)} fusion(bf16[192,8192]{1,0:T(8,128)(2,1)S(1)} %copy-done.4, bf16[40,8,64,128]{3,2,1,0:T(8,128)(2,1)S(1)} %bitcast.88), kind=kOutput, calls=%fused_computation.23 | convolution fusion | flops 1006694400 | bytes 8511488 | tf_op jit(solution)/shard_map/dot_general | solution.py:144
  140.5 10.7 %all-to-all-start = ((bf16[64,3,320]{2,1,0:T(4,128)(2,1)}), bf16[64,3,320]{2,1,0:T(4,128)(2,1)S(1)}, u32[]{:S(2)}, u32[]{:S(2)}) async-start(bf16[64,3,320]{2,1,0:T(4,128)(2,1)} %reshape.532), calls=%async_computation | async-start | bytes 393216 | tf_op jit(solution)/shard_map/all_to_all | solution.py:148
  152.0 11.8 %all-to-all-done = bf16[64,3,320]{2,1,0:T(4,128)(2,1)S(1)} async-done(((bf16[64,3,320]{2,1,0:T(4,128)(2,1)}), bf16[64,3,320]{2,1,0:T(4,128)(2,1)S(1)}, u32[]{:S(2)}, u32[]{:S(2)}) %all-to-all-start) | async-done | bytes 122912 | tf_op jit(solution)/shard_map/all_to_all | solution.py:148
  163.9 56.5 %all-gather.11.cloned.1.call-done = bf16[320,5120]{0,1:T(8,128)(2,1)} async-done(((bf16[320,80]{0,1:T(8,128)(2,1)}), bf16[320,5120]{0,1:T(8,128)(2,1)}) %all-gather.11.cloned.1.call-update) | async-done | bytes 3276816 | tf_op jit(solution)/shard_map/all_gather | solution.py:154
  220.4 5.6 %fusion.43 = f32[192,5120]{1,0:T(8,128)} fusion(bf16[320,5120]{0,1:T(8,128)(2,1)} %all-gather.11.cloned.1.call-done, f32[192,320]{1,0:T(8,128)S(1)} %reshape.539, bf16[192,1,320]{2,0,1:T(8,128)(2,1)S(1)} %copy-done.6), kind=kOutput, calls=%fused_computation.61 | convolution fusion | flops 629821440 | bytes 7577600 | tf_op jit(solution)/shard_map/dot_general | solution.py:152
  226.0 5.4 %reshape.533 = f32[64,12,1280]{2,1,0:T(8,128)} reshape(f32[192,5120]{1,0:T(8,128)} %fusion.43) | data formatting | bytes 7864320 | tf_op jit(solution)/shard_map/reshape | solution.py:162
  231.3 5.3 %convolution_convert_fusion = bf16[64,12,1280]{2,1,0:T(8,128)(2,1)S(1)} fusion(f32[64,12,1280]{2,1,0:T(8,128)} %reshape.533, s32[64,12]{1,0:T(8,128)S(1)} %copy.20, pred[64,12]{1,0:T(8,128)(4,1)S(1)} %copy.21), kind=kOutput, calls=%fused_computation.9 | convolution fusion | flops 142559232 | bytes 5902080 | tf_op jit(solution)/shard_map/spq,sqc->spc/dot_general | solution.py:159
  236.6 2.0 convert_element_type.91
  238.7 35.5 %reduce-scatter.2.cloned.1.call-done = bf16[96,1280]{1,0:T(8,128)(2,1)} async-done(((bf16[768,1280]{1,0:T(8,128)(2,1)}), bf16[96,1280]{1,0:T(8,128)(2,1)}) %reduce-scatter.2.cloned.1.call-update) | async-done | bytes 245776 | tf_op jit(solution)/shard_map/reduce_scatter | solution.py:40
  275.3 13.5 %all-to-all-start.1 = ((bf16[64,20,320]{2,1,0:T(8,128)(2,1)}), bf16[64,20,320]{2,1,0:T(8,128)(2,1)}, u32[]{:S(2)}, u32[]{:S(2)}) async-start(bf16[64,20,320]{2,1,0:T(8,128)(2,1)} %broadcast_in_dim.34), calls=%async_computation.2 | async-start | bytes 2359296 | tf_op jit(solution)/shard_map/all_to_all | solution.py:49
  289.3 2.4 multiply_reduce_fusion.1
  291.8 13.8 %all-gather.13.cloned.1.call-done = bf16[768,1280]{1,0:T(8,128)(2,1)} async-done(((bf16[96,1280]{1,0:T(8,128)(2,1)}), bf16[768,1280]{1,0:T(8,128)(2,1)}) %all-gather.13.cloned.1.call-update) | async-done | bytes 1966096 | tf_op jit(solution)/shard_map/all_gather | solution.py:43
  305.6 1.8 convert_element_type.111
  314.7 3.8 %all-to-all-done.1 = bf16[64,20,320]{2,1,0:T(8,128)(2,1)} async-done(((bf16[64,20,320]{2,1,0:T(8,128)(2,1)}), bf16[64,20,320]{2,1,0:T(8,128)(2,1)}, u32[]{:S(2)}, u32[]{:S(2)}) %all-to-all-start.1) | async-done | bytes 819232 | tf_op jit(solution)/shard_map/all_to_all | solution.py:49
  318.5 9.6 %all-to-all-start.2 = ((bf16[64,20,320]{2,1,0:T(8,128)(2,1)}), bf16[64,20,320]{2,1,0:T(8,128)(2,1)S(1)}, u32[]{:S(2)}, u32[]{:S(2)}) async-start(bf16[64,20,320]{2,1,0:T(8,128)(2,1)} %reshape.537), calls=%async_computation.3 | async-start | bytes 2359296 | tf_op jit(solution)/shard_map/all_to_all | solution.py:64
  328.2 1.5 reshape.535
  330.0 3.5 fusion.4
  333.4 2.0 fusion.42
  335.4 25.2 %all-to-all-done.2 = bf16[64,20,320]{2,1,0:T(8,128)(2,1)S(1)} async-done(((bf16[64,20,320]{2,1,0:T(8,128)(2,1)}), bf16[64,20,320]{2,1,0:T(8,128)(2,1)S(1)}, u32[]{:S(2)}, u32[]{:S(2)}) %all-to-all-start.2) | async-done | bytes 819232 | tf_op jit(solution)/shard_map/all_to_all | solution.py:64
  (80 shorter events, 19.3 us)
Async XLA Ops:
  7.2 3.1 copy-start
  7.2 5.9 %copy-start.7 = (bf16[128,320]{0,1:T(8,128)(2,1)S(1)}, bf16[128,320]{0,1:T(8,128)(2,1)}, u32[]{:S(2)}) copy-start(bf16[128,320]{0,1:T(8,128)(2,1)} %param.19) | copy-start | bytes 245764
  7.2 48.0 %all-gather.7.cloned.1.call-start = ((), (), s32[]{:S(2)}) async-start(), calls=%async_computation.4 | async-start | bytes 4718592 | tf_op jit(solution)/shard_map/all_gather | solution.py:141
  13.0 118.3 %all-gather.9.cloned.1.call-start = ((), (), s32[]{:S(2)}) async-start(), calls=%async_computation.5 | async-start | bytes 5898240 | tf_op jit(solution)/shard_map/all_gather | solution.py:20
  44.3 176.1 %all-gather.11.cloned.1.call-start = ((), (), s32[]{:S(2)}) async-start(), calls=%async_computation.6 | async-start | bytes 3993600 | tf_op jit(solution)/shard_map/all_gather | solution.py:154
  131.4 4.0 %copy-start.4 = (bf16[192,8192]{1,0:T(8,128)(2,1)S(1)}, bf16[192,8192]{1,0:T(8,128)(2,1)}, u32[]{:S(2)}) copy-start(bf16[192,8192]{1,0:T(8,128)(2,1)} %reshape.530) | copy-start | bytes 9437188
  135.4 85.0 %copy-start.6 = (bf16[192,1,320]{2,0,1:T(8,128)(2,1)S(1)}, bf16[192,1,320]{2,0,1:T(8,128)(2,1)}, u32[]{:S(2)}) copy-start(bf16[192,1,320]{2,0,1:T(8,128)(2,1)} %param.15) | copy-start | bytes 368644
  140.5 23.3 %all-to-all-start = ((bf16[64,3,320]{2,1,0:T(4,128)(2,1)}), bf16[64,3,320]{2,1,0:T(4,128)(2,1)S(1)}, u32[]{:S(2)}, u32[]{:S(2)}) async-start(bf16[64,3,320]{2,1,0:T(4,128)(2,1)} %reshape.532), calls=%async_computation | async-start | bytes 393216 | tf_op jit(solution)/shard_map/all_to_all | solution.py:148
  151.2 123.0 %reduce-scatter.2.cloned.1.call-start = ((), (), s32[]{:S(2)}) async-start(), calls=%async_computation.7 | async-start | bytes 2211840 | tf_op jit(solution)/shard_map/reduce_scatter | solution.py:40
  236.6 37.6 %copy-start.9 = (bf16[20,320]{1,0:T(8,128)(2,1)S(1)}, bf16[20,320]{1,0:T(8,128)(2,1)}, u32[]{:S(2)}) copy-start(bf16[20,320]{1,0:T(8,128)(2,1)} %param.21) | copy-start | bytes 38404
  238.7 50.2 %copy-start.3 = (bf16[768,1,1280]{2,0,1:T(8,128)(2,1)S(1)}, bf16[768,1,1280]{2,0,1:T(8,128)(2,1)}, u32[]{:S(2)}) copy-start(bf16[768,1,1280]{2,0,1:T(8,128)(2,1)} %param.16) | copy-start | bytes 5898244
  238.7 66.9 %all-gather.13.cloned.1.call-start = ((), (), s32[]{:S(2)}) async-start(), calls=%async_computation.8 | async-start | bytes 2211840 | tf_op jit(solution)/shard_map/all_gather | solution.py:43
  275.3 43.2 %all-to-all-start.1 = ((bf16[64,20,320]{2,1,0:T(8,128)(2,1)}), bf16[64,20,320]{2,1,0:T(8,128)(2,1)}, u32[]{:S(2)}, u32[]{:S(2)}) async-start(bf16[64,20,320]{2,1,0:T(8,128)(2,1)} %broadcast_in_dim.34), calls=%async_computation.2 | async-start | bytes 2359296 | tf_op jit(solution)/shard_map/all_to_all | solution.py:49
  291.7 15.7 %copy-start.8 = (f32[1280]{0:T(1024)S(1)}, f32[1280]{0:T(1024)}, u32[]{:S(2)}) copy-start(f32[1280]{0:T(1024)} %param.18) | copy-start | bytes 15364
  307.4 1.9 copy-start.2
  309.3 2.6 copy-start.10
  310.5 1.4 copy-start.5
  318.5 42.2 %all-to-all-start.2 = ((bf16[64,20,320]{2,1,0:T(8,128)(2,1)}), bf16[64,20,320]{2,1,0:T(8,128)(2,1)S(1)}, u32[]{:S(2)}, u32[]{:S(2)}) async-start(bf16[64,20,320]{2,1,0:T(8,128)(2,1)} %reshape.537), calls=%async_computation.3 | async-start | bytes 2359296 | tf_op jit(solution)/shard_map/all_to_all | solution.py:64
  329.9 31.7 %copy-start.1 = (bf16[256,1024]{1,0:T(8,128)(2,1)S(1)}, bf16[256,1024]{1,0:T(8,128)(2,1)}, u32[]{:S(2)}) copy-start(bf16[256,1024]{1,0:T(8,128)(2,1)} %param.11) | copy-start | bytes 1572868
Sparse Core Ops, SparseCore 0:
  13.2 41.9 all-gather.6
  57.2 74.1 all-gather.8
  134.4 85.9 all-gather.10
  238.8 35.3 reduce-scatter.1
  276.4 29.1 all-gather.12
where the time goes:
time: 369 us; the launch traced here: 368 us
  waiting for transfers between devices  226 us (61%)
  starting transfers between devices  34.1 us (9%)
  local copies, waits for them, and re-layouts  32 us (9%)
  blocking collectives  30.2 us (8%)
  matrix products  19.6 us (5%)
  between operations  14.1 us (4%)
  other arithmetic  11.9 us (3%)
    all_gather x1, waiting for transfers between devices, gather_in_order(): tiles = lax.all_gather(tiles, axes[k], axis=0, tiled=True)  68.7 us
    all_gather x1, waiting for transfers between devices, on_device(): lax.all_gather(merger_in_w, SEQ, axis=1, tiled=True)  56.5 us
    reduce_scatter x1, waiting for transfers between devices, sum_by_parts(): lax.psum_scatter(filled_up(lines, lax.axis_size(axis)), axis, scatter_dim...  35.5 us
    all_gather x1, blocking collectives, gather_in_order(): tiles = lax.all_gather(tiles, axes[k], axis=0, tiled=True)  30.2 us
    all_to_all x1, waiting for transfers between devices, sum_at_owner(): lax.all_to_all(tiles, axis, split_axis=0, concat_axis=0, tiled=True)  25.2 us
    all_gather x1, waiting for transfers between devices, sum_by_parts(): whole = lax.all_gather(own, axis).reshape(-1, *lines.shape[1:])  13.8 us
    all_to_all x1, starting transfers between devices, copy_for_each(): return lax.all_to_all(copies, axis, split_axis=0, concat_axis=0, tiled=True)  13.5 us
    all_to_all x1, waiting for transfers between devices, on_device(): lax.all_to_all(source_grad, SEQ, split_axis=0, concat_axis=0, tiled=True)  11.8 us
  transfers between devices with their start and end apart: 8, of which 8 were waited for; matrix products, arithmetic and copies ran while one was open for 10% of the time, Pallas kernels for 0%

commit v1 on v0

v1 whole, which is shorter than its diff:
```python
import jax
import jax.numpy as jnp
from jax import lax
from jax.experimental import pallas as pl
from jax.experimental.pallas import tpu as pltpu
from jax.sharding import Mesh
from jax.sharding import PartitionSpec as P

SLOT = 3
SEQ = ("z", "y")
GRP = ("gx", "gc")
BF16 = jnp.bfloat16
F32 = jnp.float32
PARAMS = pltpu.CompilerParams(vmem_limit_bytes=48 * 1024 * 1024)


def whole(memory=pltpu.VMEM):
    return pl.BlockSpec(memory_space=memory)


def shifted(value, axis, step):
    size = lax.axis_size(axis)
    return lax.ppermute(value, axis, [(i, (i + step) % size) for i in range(size)])


def copy_for_each(value, axis):
    copies = jnp.broadcast_to(value, (lax.axis_size(axis), *value.shape))
    return lax.all_to_all(copies, axis, split_axis=0, concat_axis=0, tiled=True)


def gelu_slope(values):
    return (
        0.5 * (1.0 + lax.erf(values * 0.7071067811865476))
        + values * jnp.exp(-0.5 * values * values) * 0.3989422804014327
    )


def hidden_kernel(order, *refs):
    pieces, (weight, out, sums) = refs[:10], refs[10:]
    w = weight[...]
    for half in range(2):
        near = pieces[5 * half : 5 * half + 5]
        for place in range(3):
            sums[order[4 * half + place]] = jnp.dot(near[place][...], w, preferred_element_type=F32)
        last = jnp.concatenate([near[3][...], near[4][...]], axis=0)
        sums[order[4 * half + 3]] = jnp.dot(last, w, preferred_element_type=F32)
    row = lax.broadcasted_iota(jnp.int32, (192, 192), 0)
    col = lax.broadcasted_iota(jnp.int32, (192, 192), 1)
    wanted = (row // 3 % 8) * 24 + (row // 24) * 3 + row % 3
    turn = jnp.where(wanted == col, 1.0, 0.0).astype(BF16)
    for part in range(8):
        block = sums[:, part * 24 : (part + 1) * 24, :].reshape(192, -1).astype(BF16)
        turned = jnp.dot(turn, block, preferred_element_type=F32)
        out[part * 8 : (part + 1) * 8] = turned.reshape(8, 24, -1).astype(BF16)


def hidden_products(order, pieces, weight):
    width = weight.shape[1]
    return pl.pallas_call(
        hidden_kernel,
        out_shape=jax.ShapeDtypeStruct((64, 24, width), BF16),
        in_specs=[whole(pltpu.SMEM)] + [whole()] * 11,
        out_specs=whole(),
        scratch_shapes=[pltpu.VMEM((8, 192, width), F32)],
        compiler_params=PARAMS,
    )(order, *pieces, weight)


def merged_kernel(core, arrived, slope, blocks, own, other, table):
    for s in range(64):
        table[s * 80 : (s + 1) * 80, :] = blocks[s, 0:80, :]
    total = arrived[0:8].astype(F32)
    for k in range(1, 8):
        total = total + arrived[8 * k : 8 * k + 8].astype(F32)
    hidden = total.reshape(192, -1).astype(BF16).astype(F32)
    grad = (slope[...] * hidden).astype(BF16)
    first = core[0] == 0
    mine = jnp.where(first, grad[:96], grad[96:])
    yours = jnp.where(first, grad[96:], grad[:96])
    dims = (((1,), (1,)), ((), ()))
    for part in range(4):
        w = table[part * 1280 : (part + 1) * 1280, :]
        own[part] = lax.dot_general(mine, w, dims, preferred_element_type=F32).astype(BF16)
        other[part] = lax.dot_general(yours, w, dims, preferred_element_type=F32).astype(BF16)


def merged_products(core, arrived, slope, blocks):
    half = jax.ShapeDtypeStruct((4, 96, 1280), BF16)
    return pl.pallas_call(
        merged_kernel,
        out_shape=(half, half),
        in_specs=[whole(pltpu.SMEM)] + [whole()] * 3,
        out_specs=(whole(), whole()),
        scratch_shapes=[pltpu.VMEM((5120, 320), BF16)],
        compiler_params=PARAMS,
    )(core, arrived, slope, blocks)


def norm_kernel(parts, inputs, gain, out):
    upstream = parts[0].astype(F32)
    for k in range(1, 4):
        upstream = upstream + parts[k].astype(F32)
    x = inputs[...].astype(F32)
    centred = x - jnp.mean(x, -1, keepdims=True)
    inverse_std = lax.rsqrt(jnp.mean(centred * centred, -1, keepdims=True) + 1e-06)
    normed = centred * inverse_std
    scaled = upstream * gain[...]
    out[...] = (
        inverse_std
        * (
            scaled
            - jnp.mean(scaled, -1, keepdims=True)
            - normed * jnp.mean(scaled * normed, -1, keepdims=True)
        )
    ).astype(BF16)


def norm_backward(parts, inputs, gain):
    return pl.pallas_call(
        norm_kernel,
        out_shape=jax.ShapeDtypeStruct((96, 1280), BF16),
        in_specs=[whole()] * 3,
        out_specs=whole(),
        compiler_params=PARAMS,
    )(parts, inputs, gain)


def on_device(
    llm_grad,
    image_grid,
    image_owner,
    row_start,
    merger_pre,
    vit_out,
    vit_pre,
    ln_gain,
    merger_out_w,
    merger_in_w,
    vit_fc2_w,
):
    x = lax.axis_index("gx")
    core = lax.axis_index("gc")
    own_index = lax.axis_index(SEQ)
    bundle = jnp.concatenate(
        [merger_in_w.T, vit_fc2_w, jnp.zeros((4, vit_fc2_w.shape[1]), BF16)], axis=0
    )
    bundles = lax.all_gather(bundle, SEQ, axis=0)

    grids = image_grid.reshape(64, 64, 2)
    counts = grids[:, :, 0] * grids[:, :, 1]
    widths = grids[:, :, 1]
    owners = image_owner.reshape(64, 64)
    starts = row_start.reshape(64, 64)
    peers = jnp.arange(64, dtype=jnp.int32)
    my_owners = lax.dynamic_index_in_dim(owners, own_index, 0, keepdims=False)
    my_counts = lax.dynamic_index_in_dim(counts, own_index, 0, keepdims=False)
    my_starts = lax.dynamic_index_in_dim(starts, own_index, 0, keepdims=False)
    targets = (my_owners[None, :] == peers[:, None]).astype(jnp.int32)
    send_counts = jnp.sum(targets * my_counts[None, :], 1)
    send_starts = jnp.sum(targets * my_starts[None, :], 1)
    within = jnp.arange(SLOT, dtype=jnp.int32)
    wanted = jnp.where(
        within[None, :] < send_counts[:, None], send_starts[:, None] + within[None, :], -1
    ).reshape(-1)
    pick = (wanted[:, None] == jnp.arange(llm_grad.shape[0], dtype=jnp.int32)[None, :]).astype(BF16)
    rows = jnp.dot(pick, llm_grad, preferred_element_type=F32).astype(BF16)

    turned = lax.ppermute(
        rows, (*GRP, "z"), [(g * 8 + z, z * 8 + g) for g in range(8) for z in range(8)]
    )
    out_w = copy_for_each(merger_out_w, "y").reshape(-1, merger_out_w.shape[1])
    left = shifted(turned, "gx", 1)
    right = shifted(turned, "gx", -1)
    far_a = shifted(left[:96], "gx", 1)
    far_b = shifted(right[96:], "gx", -1)
    near = [turned, left, right, far_a, far_b]
    pieces = near + [shifted(piece, "gc", 1) for piece in near]
    order = jnp.stack(
        [
            2 * ((x + step) % 4) + (core + flip) % 2
            for flip in (0, 1)
            for step in (0, 3, 1, 2)
        ]
    ).astype(jnp.int32)
    partial = hidden_products(order, pieces, out_w)
    arrived = lax.all_to_all(partial, SEQ, split_axis=0, concat_axis=0, tiled=True)

    pre_act = (
        merger_pre[:, 0, :].reshape(8, 8, SLOT, -1).transpose(1, 0, 2, 3).reshape(192, -1)
    )
    slope = gelu_slope(pre_act.astype(F32))
    own, other = merged_products(core.reshape(1), arrived, slope, bundles)
    swapped = shifted(other, "gc", 1)
    pair = (own.astype(F32) + swapped.astype(F32)).astype(BF16)
    parts = lax.all_to_all(pair, "gx", split_axis=0, concat_axis=0, tiled=True)

    received = (owners == own_index).astype(jnp.int32)
    recv_counts = jnp.sum(received * counts, 1)
    recv_widths = jnp.sum(received * widths, 1)
    j = jnp.arange(SLOT, dtype=jnp.int32)[None, :]
    w = recv_widths[:, None]
    base = peers[:, None] * (4 * SLOT) + (2 * (j // w)) * (2 * w) + 2 * (j % w)
    valid = j < recv_counts[:, None]
    component = jnp.arange(4, dtype=jnp.int32)[:, None, None]
    slots = base[None] + (component // 2) * (2 * w[None]) + component % 2
    slots = jnp.where(valid[None], slots, -1)
    slots = slots.reshape(4, 8, 8, SLOT).transpose(0, 2, 1, 3).reshape(4, 2, 96)
    slots = slots.transpose(1, 0, 2)
    own_slots = lax.dynamic_index_in_dim(slots, core, 0, keepdims=False)
    other_slots = lax.dynamic_index_in_dim(slots, 1 - core, 0, keepdims=False)
    places = jnp.arange(768, dtype=jnp.int32)
    mine = lax.dynamic_index_in_dim(own_slots, x, 0, keepdims=False)
    take_own = (mine[:, None] == places[None, :]).astype(BF16)
    norm_in = jnp.dot(take_own, vit_out[:, 0, :], preferred_element_type=F32).astype(BF16)
    all_slots = jnp.concatenate([own_slots.reshape(-1), other_slots.reshape(-1)])
    take_all = (all_slots[:, None] == places[None, :]).astype(BF16)
    fc_in = jnp.dot(take_all, vit_pre[:, 0, :], preferred_element_type=F32)
    sigmoid_q = jax.nn.sigmoid(1.702 * fc_in)
    activation = (fc_in * sigmoid_q).astype(BF16)
    fc_slope = sigmoid_q + 1.702 * fc_in * sigmoid_q * (1.0 - sigmoid_q)

    grad = norm_backward(parts, norm_in, ln_gain.reshape(1, -1))
    near_grad = lax.all_gather(grad, "gx", axis=0, tiled=True)
    far_grad = shifted(near_grad, "gc", 1)
    by_row = (((0,), (0,)), ((), ()))
    weight_part = lax.dot_general(
        near_grad, activation[:384], by_row, preferred_element_type=F32
    ) + lax.dot_general(far_grad, activation[384:], by_row, preferred_element_type=F32)
    sent = weight_part.astype(BF16).reshape(64, 20, -1)
    weight_grad = (
        lax.all_to_all(sent, SEQ, split_axis=0, concat_axis=0, tiled=True).astype(F32).sum(axis=0)
    )

    grads = jnp.concatenate([near_grad, far_grad], axis=0)
    fc2 = bundles[:, 80:100].reshape(1280, -1)
    act_grad = jnp.dot(grads, fc2, preferred_element_type=F32)
    fc1_rows = (fc_slope * act_grad).astype(BF16)
    fc1_grad = jnp.dot(take_all.T, fc1_rows, preferred_element_type=F32).astype(BF16)
    g = lax.axis_index(GRP)
    own_places = g * 96 + jnp.arange(96, dtype=jnp.int32)
    put_own = (own_places[:, None] == all_slots[None, :]).astype(BF16)
    own_rows = jnp.dot(put_own, grads, preferred_element_type=F32).astype(BF16)
    return (
        own_rows.reshape(96, 1, -1),
        fc1_grad.reshape(768, 1, -1),
        weight_grad,
    )


def solution(mesh):
    finer = Mesh(mesh.devices.reshape(4, 2, 8, 8), ("gx", "gc", "z", "y"))
    in_specs = (
        P(SEQ, GRP),
        P(),
        P(),
        P(),
        P(None, SEQ, GRP),
        P(None, SEQ, None),
        P(None, SEQ, GRP),
        P(),
        P(SEQ, GRP),
        P(GRP, SEQ),
        P(SEQ, GRP),
    )
    out_specs = (P(GRP, SEQ, None), P(None, SEQ, GRP), P(SEQ, GRP))
    return jax.shard_map(
        on_device, mesh=finer, in_specs=in_specs, out_specs=out_specs, check_vma=False
    )
```

time: 369 us -> 248 us (0.67)
  waiting for transfers between devices: 226 us -> 73.1 us
  starting transfers between devices: 34.1 us -> 85.2 us
  blocking collectives: 30.2 us -> 15 us
  Pallas kernels: 0 us -> 11.7 us
  local copies, waits for them, and re-layouts: 32 us -> 25.2 us
  matrix products: 19.6 us -> 13.6 us
  other arithmetic: 11.9 us -> 8 us
    all_gather x4 -> x1, waiting for transfers between devices: 149 us -> 0.01 us  [on_device(): bundles = lax.all_gather(bundle, SEQ, axis=0)]
    ppermute x0 -> x12, starting transfers between devices: none -> 54.7 us  [the longest x11 53.3 us: shifted(): lax.ppermute(value, axis, [(i, (i + step) % size) for i in range(size)])]
    reduce_scatter x1 -> x0, waiting for transfers between devices: 35.5 us -> none  [sum_by_parts(): lax.psum_scatter(filled_up(lines, lax.axis_size(axis)), axis, scatter_dim...]
    all_to_all x2 -> x3, waiting for transfers between devices: 37 us -> 66.7 us  [the longest x1 33 us: on_device(): lax.all_to_all(partial, SEQ, split_axis=0, concat_axis=0, tiled=True)]
    all_gather x1, blocking collectives: 30.2 us -> 15 us  [on_device(): near_grad = lax.all_gather(grad, 'gx', axis=0, tiled=True)]
    pallas_call x0 -> x3, Pallas kernels: none -> 11.7 us  [the longest x1 6.06 us: merged_products(): pl.pallas_call(merged_kernel, out_shape=(half, half), in_specs=[whole(plt...]
    reshape x8, local copies, waits for them, and re-layouts: 18.8 us -> 7.11 us  [the longest x1 2.28 us: on_device(): fc2 = bundles[:, 80:100].reshape(1280, -1)]
    ppermute x0 -> x12, waiting for transfers between devices: none -> 6.33 us  [the longest x11 6.33 us: shifted(): lax.ppermute(value, axis, [(i, (i + step) % size) for i in range(size)])]
  transfers between devices with their start and end apart: 8 -> 17, of which waited for: 8 -> 7; matrix products, arithmetic and copies ran while one was open for 10% -> 13% of each run, Pallas kernels for 0% -> 2%
where the time goes in v1:
time: 248 us; the launch traced here: 246 us
  starting transfers between devices  85.2 us (34%)
  waiting for transfers between devices  73.1 us (29%)
  local copies, waits for them, and re-layouts  25.2 us (10%)
  blocking collectives  15 us (6%)
  between operations  14.5 us (6%)
  matrix products  13.6 us (5%)
  Pallas kernels  11.7 us (5%)
  other arithmetic  8 us (3%)
    ppermute x11, starting transfers between devices, shifted(): lax.ppermute(value, axis, [(i, (i + step) % size) for i in range(size)])  53.3 us
    all_to_all x1, waiting for transfers between devices, on_device(): lax.all_to_all(partial, SEQ, split_axis=0, concat_axis=0, tiled=True)  33 us
    all_to_all x1, waiting for transfers between devices, on_device(): lax.all_to_all(sent, SEQ, split_axis=0, concat_axis=0, tiled=True)  19.7 us
    all_gather x1, blocking collectives, on_device(): near_grad = lax.all_gather(grad, 'gx', axis=0, tiled=True)  15 us
    all_to_all x1, waiting for transfers between devices, on_device(): parts = lax.all_to_all(pair, 'gx', split_axis=0, concat_axis=0, tiled=True)  14 us
    all_to_all x1, starting transfers between devices, copy_for_each(): return lax.all_to_all(copies, axis, split_axis=0, concat_axis=0, tiled=True)  9.91 us
    all_to_all x1, starting transfers between devices, on_device(): lax.all_to_all(partial, SEQ, split_axis=0, concat_axis=0, tiled=True)  9.38 us
    all_to_all x1, starting transfers between devices, on_device(): lax.all_to_all(sent, SEQ, split_axis=0, concat_axis=0, tiled=True)  6.99 us
  transfers between devices with their start and end apart: 17, of which 7 were waited for; matrix products, arithmetic and copies ran while one was open for 13% of the time, Pallas kernels for 2%

profile of v1, /device:TPU:8, one launch (start us, length us, event | category | flops | bytes accessed | tf_op | source)
XLA Modules:
  0.0 246.3 jit_solution(18263536749194339559)
XLA Ops:
  16.5 9.9 %all-to-all-start = ((bf16[8,128,320]{1,2,0:T(8,128)(2,1)}), bf16[8,128,320]{1,2,0:T(8,128)(2,1)}, u32[]{:S(2)}, u32[]{:S(2)}) async-start(bf16[8,128,320]{1,2,0:T(8,128)(2,1)} %broadcast_in_dim.24), calls=%async_computation | async-start | bytes 1310720 | tf_op jit(solution)/shard_map/all_to_all | solution.py:28
  26.5 29.9 %collective-permute-start.2 = (bf16[192,1024]{1,0:T(8,128)(2,1)}, bf16[192,1024]{1,0:T(8,128)(2,1)S(1)}, u32[]{:S(2)}, u32[]{:S(2)}) collective-permute-start(bf16[192,1024]{1,0:T(8,128)(2,1)} %collective-permute-done.refs_0_), channel_id=1, source_target_pairs={{0,384},{128,0},{256,128},{384,256},{1,385},{129,1},{257,129},{385... | collective-permute-start | bytes 1179656 | tf_op jit(solution)/shard_map/ppermute | solution.py:23
  60.2 5.1 %collective-permute-done.2.refs_2_ = bf16[192,1024]{1,0:T(8,128)(2,1)S(1)} collective-permute-done((bf16[192,1024]{1,0:T(8,128)(2,1)}, bf16[192,1024]{1,0:T(8,128)(2,1)S(1)}, u32[]{:S(2)}, u32[]{:S(2)}) %collective-permute-start.2) | collective-permute-done | bytes 393248 | tf_op jit(solution)/shard_map/ppermute | solution.py:23
  65.3 5.5 %collective-permute-start.4 = (bf16[96,1024]{1,0:T(8,128)(2,1)S(1)}, bf16[96,1024]{1,0:T(8,128)(2,1)}, u32[]{:S(2)}, u32[]{:S(2)}) collective-permute-start(bf16[96,1024]{1,0:T(8,128)(2,1)S(1)} %slice.32), channel_id=1, source_target_pairs={{0,384},{128,0},{256,128},{384,256},{1,385},{129,1},{257,129},{385... | collective-permute-start | bytes 589832 | tf_op jit(solution)/shard_map/ppermute | solution.py:23
  74.7 2.4 collective-permute-start.6
  83.5 5.2 %shard_map.130 = bf16[64,24,320]{2,1,0:T(8,128)(2,1)} custom-call(s32[8]{0:T(128)S(1)} %stack.35.order, bf16[192,1024]{1,0:T(8,128)(2,1)} %collective-permute-done.refs_0_, bf16[192,1024]{1,0:T(8,128)(2,1)S(1)} %collective-permute-done.1.refs_1_, bf16[192,1024]{1,0:T(8,128)(2,1)S(1)} %collective-permute-done.2.refs_2_, ...), custom_call_target="tpu_custom_call" | custom-call | tf_op jit(solution)/shard_map/pallas_call | solution.py:59
  88.7 9.4 %all-to-all-start.1 = ((bf16[64,24,320]{2,1,0:T(8,128)(2,1)}), bf16[64,24,320]{2,1,0:T(8,128)(2,1)S(1)}, u32[]{:S(2)}, u32[]{:S(2)}) async-start(bf16[64,24,320]{2,1,0:T(8,128)(2,1)} %shard_map.130), calls=%async_computation.1 | async-start | bytes 2359296 | tf_op jit(solution)/shard_map/all_to_all | solution.py:186
  102.9 33.0 %all-to-all-done.1.arrived = bf16[64,24,320]{2,1,0:T(8,128)(2,1)S(1)} async-done(((bf16[64,24,320]{2,1,0:T(8,128)(2,1)}), bf16[64,24,320]{2,1,0:T(8,128)(2,1)S(1)}, u32[]{:S(2)}, u32[]{:S(2)}) %all-to-all-start.1) | async-done | bytes 983072 | tf_op jit(solution)/shard_map/all_to_all | solution.py:186
  136.0 6.1 %shard_map.131 = (bf16[4,96,1280]{2,1,0:T(8,128)(2,1)S(1)}, bf16[4,96,1280]{2,1,0:T(8,128)(2,1)}) custom-call(s32[1]{0:T(128)} %bitcast.9.core, bf16[64,24,320]{2,1,0:T(8,128)(2,1)S(1)} %all-to-all-done.1.arrived, f32[192,320]{1,0:T(8,128)S(1)} %fusion.16.slope, bf16[64,104,320]{2,1,0:T(8,128)(2,1)} %bitcast.70), custom_call_target="tpu_custom_call" | custom-call | tf_op jit(solution)/shard_map/pallas_call | solution.py:89
  147.7 2.4 add_convert_fusion
  150.1 4.2 %all-to-all-start.2 = ((bf16[4,96,1280]{2,1,0:T(8,128)(2,1)}), bf16[4,96,1280]{2,1,0:T(8,128)(2,1)S(1)}, u32[]{:S(2)}, u32[]{:S(2)}) async-start(bf16[4,96,1280]{2,1,0:T(8,128)(2,1)} %add_convert_fusion), calls=%async_computation.2 | async-start | bytes 1966080 | tf_op jit(solution)/shard_map/all_to_all | solution.py:195
  155.1 14.0 %all-to-all-done.2.parts = bf16[4,96,1280]{2,1,0:T(8,128)(2,1)S(1)} async-done(((bf16[4,96,1280]{2,1,0:T(8,128)(2,1)}), bf16[4,96,1280]{2,1,0:T(8,128)(2,1)S(1)}, u32[]{:S(2)}, u32[]{:S(2)}) %all-to-all-start.2) | async-done | bytes 983072 | tf_op jit(solution)/shard_map/all_to_all | solution.py:195
  169.5 15.0 %all_gather.11 = bf16[384,1280]{1,0:T(8,128)(2,1)S(1)} all-gather(bf16[96,1280]{1,0:T(8,128)(2,1)S(1)} %shard_map.132), channel_id=1, replica_groups=mesh['gx'=4,'gc'=2,'z'=8,'y'=8] {'gx'}, dimensions={0}, use_global_device_ids=true | all-gather | bytes 1228800 | tf_op jit(solution)/shard_map/all_gather | solution.py:223
  184.5 2.1 collective-permute-start.11
  186.8 2.8 %multiply_convert_fusion = (bf16[768,320]{0,1:T(8,128)(2,1)S(1)}, f32[768,320]{0,1:T(8,128)}) fusion(bf16[768,1,320]{0,2,1:T(8,128)(2,1)} %param.17, s32[768]{0:T(1024)S(1)} %constant_dynamic-update-slice_fusion.3), kind=kOutput, calls=%fused_computation.18 | convolution fusion | flops 379551744 | bytes 1969152 | tf_op jit(solution)/shard_map/dot_general | solution.py:217
  190.2 2.7 %fusion = bf16[1280,320]{0,1:T(8,128)(2,1)} fusion(f32[1280,320]{0,1:T(8,128)S(1)} %fusion.19, bf16[384,1280]{1,0:T(8,128)(2,1)} %collective-permute-done.11, bf16[768,320]{0,1:T(8,128)(2,1)S(1)} %get-tuple-element.18), kind=kOutput, calls=%fused_computation.1 | convolution fusion | flops 315392000 | bytes 3686400 | tf_op jit(solution)/shard_map/dot_general | solution.py:228
  192.9 2.2 copy.42
  195.2 2.2 reshape.414
  197.4 7.0 %all-to-all-start.3 = ((bf16[64,20,320]{2,1,0:T(8,128)(2,1)}), bf16[64,20,320]{2,1,0:T(8,128)(2,1)}, u32[]{:S(2)}, u32[]{:S(2)}) async-start(bf16[64,20,320]{2,1,0:T(8,128)(2,1)} %reshape.414), calls=%async_computation.3 | async-start | bytes 2359296 | tf_op jit(solution)/shard_map/all_to_all | solution.py:231
  204.4 2.5 %slice.33 = bf16[64,20,320]{2,1,0:T(8,128)(2,1)} slice(bf16[64,104,320]{2,1,0:T(8,128)(2,1)} %bitcast.71), slice={[0:64], [80:100], [0:320]} | slice | bytes 1638400 | tf_op jit(solution)/shard_map/slice | solution.py:235
  206.9 2.3 reshape.412
  213.1 4.5 %fusion.7 = bf16[768,1,320]{0,2,1:T(8,128)(2,1)} fusion(s32[768]{0:T(1024)S(1)} %constant_dynamic-update-slice_fusion.3, bf16[768,1280]{1,0:T(8,128)(2,1)} %copy-done.2, bf16[1280,320]{1,0:T(8,128)(2,1)S(1)} %copy-done.3, f32[768,320]{0,1:T(8,128)} %get-tuple-element.19), kind=kOutput, calls=%fused_computation.15 | convolution fusion | flops 1009926144 | bytes 4262912 | tf_op jit(solution)/shard_map/dot_general | solution.py:238
  217.6 19.7 %all-to-all-done.3 = bf16[64,20,320]{2,1,0:T(8,128)(2,1)} async-done(((bf16[64,20,320]{2,1,0:T(8,128)(2,1)}), bf16[64,20,320]{2,1,0:T(8,128)(2,1)}, u32[]{:S(2)}, u32[]{:S(2)}) %all-to-all-start.3) | async-done | bytes 819232 | tf_op jit(solution)/shard_map/all_to_all | solution.py:231
  237.3 2.1 convert_reduce_fusion
  (106 shorter events, 39.6 us)
Async XLA Ops:
  7.2 147.4 %copy-start = (bf16[768,1,1280]{2,0,1:T(8,128)(2,1)S(1)}, bf16[768,1,1280]{2,0,1:T(8,128)(2,1)}, u32[]{:S(2)}) copy-start(bf16[768,1,1280]{2,0,1:T(8,128)(2,1)} %param.16) | copy-start | bytes 5898244
  7.2 128.8 %all-gather.3.cloned.1.call-start = ((), (), s32[]{:S(2)}) async-start(), calls=%async_computation.4 | async-start | bytes 5191680 | tf_op jit(solution)/shard_map/all_gather | solution.py:147
  13.3 13.2 %collective-permute-start = (bf16[192,1024]{1,0:T(8,128)(2,1)S(1)}, bf16[192,1024]{1,0:T(8,128)(2,1)}, u32[]{:S(2)}, u32[]{:S(2)}) collective-permute-start(bf16[192,1024]{1,0:T(8,128)(2,1)S(1)} %convolution_convert_fusion.2), channel_id=1, source_target_pairs={{0,0},{8,64},{16,128},{24,192},{32,256},{40,320},{48,384},{56,448}... | collective-permute-start | bytes 1179656 | tf_op jit(solution)/shard_map/ppermute | solution.py:168
  16.5 65.3 %all-to-all-start = ((bf16[8,128,320]{1,2,0:T(8,128)(2,1)}), bf16[8,128,320]{1,2,0:T(8,128)(2,1)}, u32[]{:S(2)}, u32[]{:S(2)}) async-start(bf16[8,128,320]{1,2,0:T(8,128)(2,1)} %broadcast_in_dim.24), calls=%async_computation | async-start | bytes 1310720 | tf_op jit(solution)/shard_map/all_to_all | solution.py:28
  26.5 38.8 %collective-permute-start.2 = (bf16[192,1024]{1,0:T(8,128)(2,1)}, bf16[192,1024]{1,0:T(8,128)(2,1)S(1)}, u32[]{:S(2)}, u32[]{:S(2)}) collective-permute-start(bf16[192,1024]{1,0:T(8,128)(2,1)} %collective-permute-done.refs_0_), channel_id=1, source_target_pairs={{0,384},{128,0},{256,128},{384,256},{1,385},{129,1},{257,129},{385... | collective-permute-start | bytes 1179656 | tf_op jit(solution)/shard_map/ppermute | solution.py:23
  56.3 14.5 %collective-permute-start.1 = (bf16[192,1024]{1,0:T(8,128)(2,1)}, bf16[192,1024]{1,0:T(8,128)(2,1)S(1)}, u32[]{:S(2)}, u32[]{:S(2)}) collective-permute-start(bf16[192,1024]{1,0:T(8,128)(2,1)} %collective-permute-done.refs_0_), channel_id=1, source_target_pairs={{0,128},{128,256},{256,384},{384,0},{1,129},{129,257},{257,385},{3... | collective-permute-start | bytes 1179656 | tf_op jit(solution)/shard_map/ppermute | solution.py:23
  58.2 25.1 %collective-permute-start.5 = (bf16[192,1024]{1,0:T(8,128)(2,1)}, bf16[192,1024]{1,0:T(8,128)(2,1)}, u32[]{:S(2)}, u32[]{:S(2)}) collective-permute-start(bf16[192,1024]{1,0:T(8,128)(2,1)} %collective-permute-done.refs_0_), channel_id=1, source_target_pairs={{0,64},{64,0},{1,65},{65,1},{2,66},{66,2},{3,67},{67,3},{4,68},{68... | collective-permute-start | bytes 1179656 | tf_op jit(solution)/shard_map/ppermute | solution.py:23
  65.3 11.8 %collective-permute-start.4 = (bf16[96,1024]{1,0:T(8,128)(2,1)S(1)}, bf16[96,1024]{1,0:T(8,128)(2,1)}, u32[]{:S(2)}, u32[]{:S(2)}) collective-permute-start(bf16[96,1024]{1,0:T(8,128)(2,1)S(1)} %slice.32), channel_id=1, source_target_pairs={{0,384},{128,0},{256,128},{384,256},{1,385},{129,1},{257,129},{385... | collective-permute-start | bytes 589832 | tf_op jit(solution)/shard_map/ppermute | solution.py:23
  70.8 9.0 %collective-permute-start.3 = (bf16[96,1024]{1,0:T(8,128)(2,1)S(1)}, bf16[96,1024]{1,0:T(8,128)(2,1)}, u32[]{:S(2)}, u32[]{:S(2)}) collective-permute-start(bf16[96,1024]{1,0:T(8,128)(2,1)S(1)} %slice.31), channel_id=1, source_target_pairs={{0,128},{128,256},{256,384},{384,0},{1,129},{129,257},{257,385},{3... | collective-permute-start | bytes 589832 | tf_op jit(solution)/shard_map/ppermute | solution.py:23
  72.7 10.6 %collective-permute-start.7 = (bf16[192,1024]{1,0:T(8,128)(2,1)S(1)}, bf16[192,1024]{1,0:T(8,128)(2,1)}, u32[]{:S(2)}, u32[]{:S(2)}) collective-permute-start(bf16[192,1024]{1,0:T(8,128)(2,1)S(1)} %collective-permute-done.2.refs_2_), channel_id=1, source_target_pairs={{0,64},{64,0},{1,65},{65,1},{2,66},{66,2},{3,67},{67,3},{4,68},{68... | collective-permute-start | bytes 1179656 | tf_op jit(solution)/shard_map/ppermute | solution.py:23
  74.7 8.8 %collective-permute-start.6 = (bf16[192,1024]{1,0:T(8,128)(2,1)S(1)}, bf16[192,1024]{1,0:T(8,128)(2,1)}, u32[]{:S(2)}, u32[]{:S(2)}) collective-permute-start(bf16[192,1024]{1,0:T(8,128)(2,1)S(1)} %collective-permute-done.1.refs_1_), channel_id=1, source_target_pairs={{0,64},{64,0},{1,65},{65,1},{2,66},{66,2},{3,67},{67,3},{4,68},{68... | collective-permute-start | bytes 1179656 | tf_op jit(solution)/shard_map/ppermute | solution.py:23
  77.1 6.3 %collective-permute-start.9 = (bf16[96,1024]{1,0:T(8,128)(2,1)}, bf16[96,1024]{1,0:T(8,128)(2,1)}, u32[]{:S(2)}, u32[]{:S(2)}) collective-permute-start(bf16[96,1024]{1,0:T(8,128)(2,1)} %collective-permute-done.4.refs_4_), channel_id=1, source_target_pairs={{0,64},{64,0},{1,65},{65,1},{2,66},{66,2},{3,67},{67,3},{4,68},{68... | collective-permute-start | bytes 589832 | tf_op jit(solution)/shard_map/ppermute | solution.py:23
  79.8 3.7 %collective-permute-start.8 = (bf16[96,1024]{1,0:T(8,128)(2,1)}, bf16[96,1024]{1,0:T(8,128)(2,1)}, u32[]{:S(2)}, u32[]{:S(2)}) collective-permute-start(bf16[96,1024]{1,0:T(8,128)(2,1)} %collective-permute-done.3.refs_3_), channel_id=1, source_target_pairs={{0,64},{64,0},{1,65},{65,1},{2,66},{66,2},{3,67},{67,3},{4,68},{68... | collective-permute-start | bytes 589832 | tf_op jit(solution)/shard_map/ppermute | solution.py:23
  88.6 9.4 %copy-start.4 = (f32[1280]{0:T(1024)S(1)}, f32[1280]{0:T(1024)}, u32[]{:S(2)}) copy-start(f32[1280]{0:T(1024)} %param.18) | copy-start | bytes 15364
  88.7 47.3 %all-to-all-start.1 = ((bf16[64,24,320]{2,1,0:T(8,128)(2,1)}), bf16[64,24,320]{2,1,0:T(8,128)(2,1)S(1)}, u32[]{:S(2)}, u32[]{:S(2)}) async-start(bf16[64,24,320]{2,1,0:T(8,128)(2,1)} %shard_map.130), calls=%async_computation.1 | async-start | bytes 2359296 | tf_op jit(solution)/shard_map/all_to_all | solution.py:186
  142.1 1.0 copy-start.1
  143.0 4.7 %collective-permute-start.10 = (bf16[4,96,1280]{2,1,0:T(8,128)(2,1)}, bf16[4,96,1280]{2,1,0:T(8,128)(2,1)S(1)}, u32[]{:S(2)}, u32[]{:S(2)}) collective-permute-start(bf16[4,96,1280]{2,1,0:T(8,128)(2,1)} %get-tuple-element.6), channel_id=1, source_target_pairs={{0,64},{64,0},{1,65},{65,1},{2,66},{66,2},{3,67},{67,3},{4,68},{68... | collective-permute-start | bytes 2949128 | tf_op jit(solution)/shard_map/ppermute | solution.py:23
  150.1 18.9 %all-to-all-start.2 = ((bf16[4,96,1280]{2,1,0:T(8,128)(2,1)}), bf16[4,96,1280]{2,1,0:T(8,128)(2,1)S(1)}, u32[]{:S(2)}, u32[]{:S(2)}) async-start(bf16[4,96,1280]{2,1,0:T(8,128)(2,1)} %add_convert_fusion), calls=%async_computation.2 | async-start | bytes 1966080 | tf_op jit(solution)/shard_map/all_to_all | solution.py:195
  184.5 5.7 %collective-permute-start.11 = (bf16[384,1280]{1,0:T(8,128)(2,1)S(1)}, bf16[384,1280]{1,0:T(8,128)(2,1)}, u32[]{:S(2)}, u32[]{:S(2)}) collective-permute-start(bf16[384,1280]{1,0:T(8,128)(2,1)S(1)} %all_gather.11), channel_id=1, source_target_pairs={{0,64},{64,0},{1,65},{65,1},{2,66},{66,2},{3,67},{67,3},{4,68},{68... | collective-permute-start | bytes 2949128 | tf_op jit(solution)/shard_map/ppermute | solution.py:23
  197.4 39.9 %all-to-all-start.3 = ((bf16[64,20,320]{2,1,0:T(8,128)(2,1)}), bf16[64,20,320]{2,1,0:T(8,128)(2,1)}, u32[]{:S(2)}, u32[]{:S(2)}) async-start(bf16[64,20,320]{2,1,0:T(8,128)(2,1)} %reshape.414), calls=%async_computation.3 | async-start | bytes 2359296 | tf_op jit(solution)/shard_map/all_to_all | solution.py:231
  209.2 3.9 %copy-start.3 = (bf16[1280,320]{1,0:T(8,128)(2,1)S(1)}, bf16[1280,320]{1,0:T(8,128)(2,1)}, u32[]{:S(2)}) copy-start(bf16[1280,320]{1,0:T(8,128)(2,1)} %reshape.412) | copy-start | bytes 2457604
  210.6 1.3 copy-start.2
Sparse Core Ops, SparseCore 0:
  11.6 117.5 all-gather.2

commit v2 on v1

v2 whole, which is shorter than its diff:
```python
import jax
import jax.numpy as jnp
from jax import lax
from jax.experimental import pallas as pl
from jax.experimental.pallas import tpu as pltpu
from jax.sharding import Mesh
from jax.sharding import PartitionSpec as P

SLOT = 3
SEQ = ("z", "y")
GRP = ("gx", "gc")
BF16 = jnp.bfloat16
F32 = jnp.float32
PARAMS = pltpu.CompilerParams(vmem_limit_bytes=48 * 1024 * 1024)


def whole(memory=pltpu.VMEM):
    return pl.BlockSpec(memory_space=memory)


def shifted(value, axis, step):
    size = lax.axis_size(axis)
    return lax.ppermute(value, axis, [(i, (i + step) % size) for i in range(size)])


def gelu_slope(values):
    return (
        0.5 * (1.0 + lax.erf(values * 0.7071067811865476))
        + values * jnp.exp(-0.5 * values * values) * 0.3989422804014327
    )


def hidden_kernel(order, *refs):
    pieces, (near, far, out, sums, table) = refs[:5], refs[5:]
    last = jnp.concatenate([pieces[3][...], pieces[4][...]], axis=0)
    for core, weight in enumerate((near, far)):
        for k in range(8):
            table[k * 128 : (k + 1) * 128, :] = weight[k, 0:128, :]
        w = table[...]
        for place in range(4):
            rows = pieces[place][...] if place < 3 else last
            sums[order[place] + 4 * core] = jnp.dot(rows, w, preferred_element_type=F32)
    row = lax.broadcasted_iota(jnp.int32, (192, 192), 0)
    col = lax.broadcasted_iota(jnp.int32, (192, 192), 1)
    wanted = (row // 3 % 8) * 24 + (row // 24) * 3 + row % 3
    turn = jnp.where(wanted == col, 1.0, 0.0).astype(BF16)
    for part in range(8):
        block = sums[:, part * 24 : (part + 1) * 24, :].reshape(192, -1).astype(BF16)
        turned = jnp.dot(turn, block, preferred_element_type=F32)
        out[part * 8 : (part + 1) * 8] = turned.reshape(8, 24, -1).astype(BF16)


def hidden_products(order, pieces, near, far):
    width = near.shape[2]
    return pl.pallas_call(
        hidden_kernel,
        out_shape=jax.ShapeDtypeStruct((64, 24, width), BF16),
        in_specs=[whole(pltpu.SMEM)] + [whole()] * 7,
        out_specs=whole(),
        scratch_shapes=[pltpu.VMEM((8, 192, width), F32), pltpu.VMEM((1024, width), BF16)],
        compiler_params=PARAMS,
    )(order, *pieces, near, far)


def sum_kernel(arrived, keep, send):
    total = arrived[0:8].astype(F32)
    for k in range(1, 8):
        total = total + arrived[8 * k : 8 * k + 8].astype(F32)
    hidden = total.reshape(192, -1).astype(BF16)
    row = lax.broadcasted_iota(jnp.int32, (96, 192), 0)
    col = lax.broadcasted_iota(jnp.int32, (96, 192), 1)
    first = row // 12 * 24 + row % 12
    for half, out in enumerate((keep, send)):
        pick = jnp.where(first + 12 * half == col, 1.0, 0.0).astype(BF16)
        out[...] = jnp.dot(pick, hidden, preferred_element_type=F32).astype(BF16)


def hidden_sums(arrived):
    half = jax.ShapeDtypeStruct((96, arrived.shape[2]), BF16)
    return pl.pallas_call(
        sum_kernel,
        out_shape=(half, half),
        in_specs=[whole()],
        out_specs=(whole(), whole()),
        compiler_params=PARAMS,
    )(arrived)


def merged_kernel(kept, received, slope, table, own, other):
    hidden = jnp.concatenate([kept[...], received[...]], axis=0).astype(F32)
    grad = (slope[...] * hidden).astype(BF16)
    dims = (((1,), (1,)), ((), ()))
    for part in range(4):
        w = table[part * 1280 : (part + 1) * 1280, :]
        both = lax.dot_general(grad, w, dims, preferred_element_type=F32).astype(BF16)
        own[part] = both[:96]
        other[part] = both[96:]


def merged_products(kept, received, slope, table):
    half = jax.ShapeDtypeStruct((4, 96, 1280), BF16)
    return pl.pallas_call(
        merged_kernel,
        out_shape=(half, half),
        in_specs=[whole()] * 4,
        out_specs=(whole(), whole()),
        compiler_params=PARAMS,
    )(kept, received, slope, table)


def norm_kernel(parts, inputs, gain, out):
    upstream = parts[0].astype(F32)
    for k in range(1, 4):
        upstream = upstream + parts[k].astype(F32)
    x = inputs[...].astype(F32)
    centred = x - jnp.mean(x, -1, keepdims=True)
    inverse_std = lax.rsqrt(jnp.mean(centred * centred, -1, keepdims=True) + 1e-06)
    normed = centred * inverse_std
    scaled = upstream * gain[...]
    out[...] = (
        inverse_std
        * (
            scaled
            - jnp.mean(scaled, -1, keepdims=True)
            - normed * jnp.mean(scaled * normed, -1, keepdims=True)
        )
    ).astype(BF16)


def norm_backward(parts, inputs, gain):
    return pl.pallas_call(
        norm_kernel,
        out_shape=jax.ShapeDtypeStruct((96, 1280), BF16),
        in_specs=[whole()] * 3,
        out_specs=whole(),
        compiler_params=PARAMS,
    )(parts, inputs, gain)


def weight_kernel(near, far, activation, out, total, turned, packed):
    dims = (((0,), (0,)), ((), ()))
    total[:, 256:384] = jnp.zeros((1280, 128), F32)
    total[:, 0:320] = lax.dot_general(
        near[...], activation[0:384, :], dims, preferred_element_type=F32
    ) + lax.dot_general(far[...], activation[384:768, :], dims, preferred_element_type=F32)
    turned[...] = pltpu.roll(total[:, 256:384], 64, 1)
    for s in range(64):
        row = s * 20
        packed[s, 0:20, :] = total[row : row + 20, 0:128]
        packed[s, 20:40, :] = total[row : row + 20, 128:256]
        packed[s, 40:50, :] = total[row : row + 10, 256:384] + turned[row + 10 : row + 20, :]
        packed[s, 50:56, :] = jnp.zeros((6, 128), F32)
    out[...] = packed[...].astype(BF16)


def weight_products(near, far, activation):
    return pl.pallas_call(
        weight_kernel,
        out_shape=jax.ShapeDtypeStruct((64, 56, 128), BF16),
        in_specs=[whole()] * 3,
        out_specs=whole(),
        scratch_shapes=[
            pltpu.VMEM((1280, 384), F32),
            pltpu.VMEM((1280, 128), F32),
            pltpu.VMEM((64, 56, 128), F32),
        ],
        compiler_params=PARAMS,
    )(near, far, activation)


def unpack_kernel(arrived, out, total, turned):
    total[...] = jnp.sum(arrived[...].astype(F32), axis=0)
    turned[...] = pltpu.roll(total[...], 64, 1)
    out[:, 0:128] = total[0:20, :]
    out[:, 128:256] = total[20:40, :]
    out[0:10, 256:320] = total[40:50, 0:64]
    out[10:20, 256:320] = turned[40:50, 0:64]


def weight_sums(arrived):
    return pl.pallas_call(
        unpack_kernel,
        out_shape=jax.ShapeDtypeStruct((20, 320), F32),
        in_specs=[whole()],
        out_specs=whole(),
        scratch_shapes=[pltpu.VMEM((56, 128), F32), pltpu.VMEM((56, 128), F32)],
        compiler_params=PARAMS,
    )(arrived)


def on_device(
    llm_grad,
    image_grid,
    image_owner,
    row_start,
    merger_pre,
    vit_out,
    vit_pre,
    ln_gain,
    merger_out_w,
    merger_in_w,
    vit_fc2_w,
):
    x = lax.axis_index("gx")
    core = lax.axis_index("gc")
    own_index = lax.axis_index(SEQ)
    peers = jnp.arange(64, dtype=jnp.int32)
    my_owners = lax.dynamic_slice_in_dim(image_owner, own_index * 64, 64)
    my_starts = lax.dynamic_slice_in_dim(row_start, own_index * 64, 64)
    my_grids = lax.dynamic_slice_in_dim(image_grid, own_index * 64, 64)
    my_counts = my_grids[:, 0] * my_grids[:, 1]
    targets = (my_owners[None, :] == peers[:, None]).astype(jnp.int32)
    send_counts = jnp.sum(targets * my_counts[None, :], 1)
    send_starts = jnp.sum(targets * my_starts[None, :], 1)
    within = jnp.arange(SLOT, dtype=jnp.int32)
    wanted = jnp.where(
        within[None, :] < send_counts[:, None], send_starts[:, None] + within[None, :], -1
    ).reshape(-1)
    pick = (wanted[:, None] == jnp.arange(llm_grad.shape[0], dtype=jnp.int32)[None, :]).astype(BF16)
    rows = jnp.dot(pick, llm_grad, preferred_element_type=F32).astype(BF16)

    fc2_rows = jnp.pad(vit_fc2_w, ((0, 12), (0, 0)))
    rows, fc2_rows = lax.optimization_barrier((rows, fc2_rows))
    along_y = lax.all_gather(jnp.concatenate([merger_out_w, fc2_rows], axis=0), "y", axis=0)
    turned = lax.ppermute(
        rows, (*GRP, "z"), [(g * 8 + z, z * 8 + g) for g in range(8) for z in range(8)]
    )
    turned, along_y = lax.optimization_barrier((turned, along_y))
    across = shifted(along_y, "gc", 1)
    left = shifted(turned, "gx", 1)
    right = shifted(turned, "gx", -1)
    far_a = shifted(left[:96], "gx", 1)
    far_b = shifted(right[96:], "gx", -1)
    pieces = [turned, left, right, far_a, far_b]
    order = jnp.stack([(x + step) % 4 for step in (0, 3, 1, 2)]).astype(jnp.int32)
    partial = hidden_products(order, pieces, along_y, across)
    partial, merger_pre, image_owner, image_grid, vit_pre, vit_out = lax.optimization_barrier(
        (partial, merger_pre, image_owner, image_grid, vit_pre, vit_out)
    )
    arrived = lax.all_to_all(partial, SEQ, split_axis=0, concat_axis=0, tiled=True)

    pre_act = merger_pre[:, 0, :].reshape(4, 2, 8, SLOT, -1).transpose(1, 2, 0, 3, 4)
    pre_act = pre_act.reshape(2, 96, -1)
    pre_act = jnp.where(core == 0, pre_act, pre_act[::-1]).reshape(192, -1)
    slope = gelu_slope(pre_act.astype(F32))
    table = lax.all_gather(merger_in_w.T, SEQ, axis=0, tiled=True)
    fc2_y = along_y[:, 128:, :].reshape(256, -1)
    fc2 = lax.all_gather(fc2_y, "z", axis=0, tiled=True)
    kept, passed = hidden_sums(arrived)
    own, other = merged_products(kept, shifted(passed, "gc", 1), slope, table)
    swapped = shifted(other, "gc", 1)
    pair = (own.astype(F32) + swapped.astype(F32)).astype(BF16)
    parts = lax.all_to_all(pair, "gx", split_axis=0, concat_axis=0, tiled=True)

    grids = image_grid.reshape(64, 64, 2)
    counts = grids[:, :, 0] * grids[:, :, 1]
    widths = grids[:, :, 1]
    owners = image_owner.reshape(64, 64)
    received = (owners == own_index).astype(jnp.int32)
    recv_counts = jnp.sum(received * counts, 1)
    recv_widths = jnp.sum(received * widths, 1)
    j = jnp.arange(SLOT, dtype=jnp.int32)[None, :]
    w = recv_widths[:, None]
    base = peers[:, None] * (4 * SLOT) + (2 * (j // w)) * (2 * w) + 2 * (j % w)
    valid = j < recv_counts[:, None]
    component = jnp.arange(4, dtype=jnp.int32)[:, None, None]
    slots = base[None] + (component // 2) * (2 * w[None]) + component % 2
    slots = jnp.where(valid[None], slots, -1)
    slots = slots.reshape(4, 4, 2, 8, SLOT).transpose(2, 0, 3, 1, 4).reshape(2, 4, 96)
    own_slots = lax.dynamic_index_in_dim(slots, core, 0, keepdims=False)
    other_slots = lax.dynamic_index_in_dim(slots, 1 - core, 0, keepdims=False)
    places = jnp.arange(768, dtype=jnp.int32)
    mine = lax.dynamic_index_in_dim(own_slots, x, 0, keepdims=False)
    take_own = (mine[:, None] == places[None, :]).astype(BF16)
    norm_in = jnp.dot(take_own, vit_out[:, 0, :], preferred_element_type=F32).astype(BF16)
    all_slots = jnp.concatenate([own_slots.reshape(-1), other_slots.reshape(-1)])
    take_all = (all_slots[:, None] == places[None, :]).astype(BF16)
    fc_in = jnp.dot(take_all, vit_pre[:, 0, :], preferred_element_type=F32)
    sigmoid_q = jax.nn.sigmoid(1.702 * fc_in)
    activation = (fc_in * sigmoid_q).astype(BF16)
    fc_slope = sigmoid_q + 1.702 * fc_in * sigmoid_q * (1.0 - sigmoid_q)

    grad = norm_backward(parts, norm_in, ln_gain.reshape(1, -1))
    near_grad = lax.all_gather(grad, "gx", axis=0, tiled=True)
    far_grad = shifted(near_grad, "gc", 1)
    sent = weight_products(near_grad, far_grad, activation)
    weight_grad = weight_sums(
        lax.all_to_all(sent, SEQ, split_axis=0, concat_axis=0, tiled=True)
    )

    grads = jnp.concatenate([near_grad, far_grad], axis=0)
    fc2 = fc2.reshape(64, 32, -1)[:, :20].reshape(1280, -1)
    act_grad = jnp.dot(grads, fc2, preferred_element_type=F32)
    fc1_rows = (fc_slope * act_grad).astype(BF16)
    fc1_grad = jnp.dot(take_all.T, fc1_rows, preferred_element_type=F32).astype(BF16)
    g = lax.axis_index(GRP)
    own_places = g * 96 + jnp.arange(96, dtype=jnp.int32)
    put_own = (own_places[:, None] == all_slots[None, :]).astype(BF16)
    own_rows = jnp.dot(put_own, grads, preferred_element_type=F32).astype(BF16)
    return (
        own_rows.reshape(96, 1, -1),
        fc1_grad.reshape(768, 1, -1),
        weight_grad,
    )


def solution(mesh):
    finer = Mesh(mesh.devices.reshape(4, 2, 8, 8), ("gx", "gc", "z", "y"))
    in_specs = (
        P(SEQ, GRP),
        P(),
        P(),
        P(),
        P(None, SEQ, GRP),
        P(None, SEQ, None),
        P(None, SEQ, GRP),
        P(),
        P(SEQ, GRP),
        P(GRP, SEQ),
        P(SEQ, GRP),
    )
    out_specs = (P(GRP, SEQ, None), P(None, SEQ, GRP), P(SEQ, GRP))
    return jax.shard_map(
        on_device, mesh=finer, in_specs=in_specs, out_specs=out_specs, check_vma=False
    )
```

time: 248 us -> 240 us (0.968)
  blocking collectives: 15 us -> 44.8 us
  starting transfers between devices: 85.2 us -> 55.9 us
  other arithmetic: 8 us -> 3.29 us
  Pallas kernels: 11.7 us -> 15.4 us
  local copies, waits for them, and re-layouts: 25.2 us -> 21.5 us
    all_gather x0 -> x1, blocking collectives: none -> 29.8 us  [on_device(): lax.all_gather(jnp.concatenate([merger_out_w, fc2_rows], axis=0), 'y', ax...]
    ppermute x11 -> x8, starting transfers between devices: 53.3 us -> 28.8 us  [shifted(): lax.ppermute(value, axis, [(i, (i + step) % size) for i in range(size)])]
    all_to_all x1 -> x0, starting transfers between devices: 9.91 us -> none  [copy_for_each(): return lax.all_to_all(copies, axis, split_axis=0, concat_axis=0, tiled=True)]
    ppermute x11 -> x8, waiting for transfers between devices: 6.33 us -> 13.2 us  [shifted(): lax.ppermute(value, axis, [(i, (i + step) % size) for i in range(size)])]
    convert_element_type x4 -> x0, local copies, waits for them, and re-layouts: 5.92 us -> none  [the longest x3 3.71 us: on_device(): slope = gelu_slope(pre_act.astype(F32))]
    all_to_all x1, waiting for transfers between devices: 19.7 us -> 13.8 us  [on_device(): lax.all_to_all(sent, SEQ, split_axis=0, concat_axis=0, tiled=True)]
    pallas_call x1 -> x4, Pallas kernels: 6.06 us -> 11.2 us  [the longest x1 4.68 us: merged_products(): pl.pallas_call(merged_kernel, out_shape=(half, half), in_specs=[whole()]...]
    all_to_all x1, starting transfers between devices: 9.38 us -> 14.1 us  [on_device(): lax.all_to_all(partial, SEQ, split_axis=0, concat_axis=0, tiled=True)]
  transfers between devices with their start and end apart: 17 -> 14, of which waited for: 7 -> 7; matrix products, arithmetic and copies ran while one was open for 13% -> 12% of each run, Pallas kernels for 2% -> 6%
where the time goes in v2:
time: 240 us; the launch traced here: 239 us
  waiting for transfers between devices  71.7 us (30%)
  starting transfers between devices  55.9 us (23%)
  blocking collectives  44.8 us (19%)
  local copies, waits for them, and re-layouts  21.5 us (9%)
  Pallas kernels  15.4 us (6%)
  between operations  14.6 us (6%)
  matrix products  11.3 us (5%)
  other arithmetic  3.29 us (1%)
    all_gather x1, blocking collectives, on_device(): lax.all_gather(jnp.concatenate([merger_out_w, fc2_rows], axis=0), 'y', ax...  29.8 us
    all_to_all x1, waiting for transfers between devices, on_device(): lax.all_to_all(partial, SEQ, split_axis=0, concat_axis=0, tiled=True)  29.7 us
    ppermute x8, starting transfers between devices, shifted(): lax.ppermute(value, axis, [(i, (i + step) % size) for i in range(size)])  28.8 us
    all_gather x1, blocking collectives, on_device(): near_grad = lax.all_gather(grad, 'gx', axis=0, tiled=True)  15 us
    all_to_all x1, waiting for transfers between devices, on_device(): parts = lax.all_to_all(pair, 'gx', split_axis=0, concat_axis=0, tiled=True)  14.3 us
    all_to_all x1, starting transfers between devices, on_device(): lax.all_to_all(partial, SEQ, split_axis=0, concat_axis=0, tiled=True)  14.1 us
    all_to_all x1, waiting for transfers between devices, on_device(): lax.all_to_all(sent, SEQ, split_axis=0, concat_axis=0, tiled=True)  13.8 us
    ppermute x8, waiting for transfers between devices, shifted(): lax.ppermute(value, axis, [(i, (i + step) % size) for i in range(size)])  13.2 us
  transfers between devices with their start and end apart: 14, of which 7 were waited for; matrix products, arithmetic and copies ran while one was open for 12% of the time, Pallas kernels for 6%

profile of v2, /device:TPU:8, one launch (start us, length us, event | category | flops | bytes accessed | tf_op | source)
XLA Modules:
  0.0 238.5 jit_solution(64861060327908)
XLA Ops:
  11.3 2.1 convolution_convert_fusion.2
  15.2 29.8 %all-gather = bf16[1280,320]{1,0:T(8,128)(2,1)S(1)} all-gather(bf16[160,320]{1,0:T(8,128)(2,1)S(1)} %pad_maximum_fusion), channel_id=2, replica_groups=mesh['gx'=4,'gc'=2,'z'=8,'y'=8] {'y'}, dimensions={0}, use_global_device_ids=true | all-gather | bytes 921600 | tf_op jit(solution)/shard_map/all_gather | solution.py:224
  47.6 6.1 %collective-permute-start.1 = (bf16[192,1024]{1,0:T(8,128)(2,1)}, bf16[192,1024]{1,0:T(8,128)(2,1)S(1)}, u32[]{:S(2)}, u32[]{:S(2)}) collective-permute-start(bf16[192,1024]{1,0:T(8,128)(2,1)} %copy-done.5), channel_id=1, source_target_pairs={{0,128},{128,256},{256,384},{384,0},{1,129},{129,257},{257,385},{3... | collective-permute-start | bytes 1179656 | tf_op jit(solution)/shard_map/ppermute | solution.py:23
  53.8 7.6 %collective-permute-start.2 = (bf16[192,1024]{1,0:T(8,128)(2,1)}, bf16[192,1024]{1,0:T(8,128)(2,1)S(1)}, u32[]{:S(2)}, u32[]{:S(2)}) collective-permute-start(bf16[192,1024]{1,0:T(8,128)(2,1)} %copy-done.5), channel_id=1, source_target_pairs={{0,384},{128,0},{256,128},{384,256},{1,385},{129,1},{257,129},{385... | collective-permute-start | bytes 1179656 | tf_op jit(solution)/shard_map/ppermute | solution.py:23
  61.4 8.0 %collective-permute-done.1.refs_1_ = bf16[192,1024]{1,0:T(8,128)(2,1)S(1)} collective-permute-done((bf16[192,1024]{1,0:T(8,128)(2,1)}, bf16[192,1024]{1,0:T(8,128)(2,1)S(1)}, u32[]{:S(2)}, u32[]{:S(2)}) %collective-permute-start.1) | collective-permute-done | bytes 393248 | tf_op jit(solution)/shard_map/ppermute | solution.py:23
  73.6 5.1 %collective-permute-start.4 = (bf16[96,1024]{1,0:T(8,128)(2,1)}, bf16[96,1024]{1,0:T(8,128)(2,1)}, u32[]{:S(2)}, u32[]{:S(2)}) collective-permute-start(bf16[96,1024]{1,0:T(8,128)(2,1)} %slice.34), channel_id=1, source_target_pairs={{0,384},{128,0},{256,128},{384,256},{1,385},{129,1},{257,129},{385... | collective-permute-start | bytes 589832 | tf_op jit(solution)/shard_map/ppermute | solution.py:23
  80.2 2.8 %collective-permute-done.4.refs_4_ = bf16[96,1024]{1,0:T(8,128)(2,1)} collective-permute-done((bf16[96,1024]{1,0:T(8,128)(2,1)}, bf16[96,1024]{1,0:T(8,128)(2,1)}, u32[]{:S(2)}, u32[]{:S(2)}) %collective-permute-start.4) | collective-permute-done | bytes 196640 | tf_op jit(solution)/shard_map/ppermute | solution.py:23
  84.9 3.8 %shard_map.130 = bf16[64,24,320]{2,1,0:T(8,128)(2,1)S(1)} custom-call(s32[4]{0:T(128)S(1)} %pad_add_fusion.order, bf16[192,1024]{1,0:T(8,128)(2,1)S(1)} %copy-done.6, bf16[192,1024]{1,0:T(8,128)(2,1)S(1)} %collective-permute-done.1.refs_1_, bf16[192,1024]{1,0:T(8,128)(2,1)S(1)} %copy-done.4, bf16[96,1024]{1,0:T(8,128)(2,1)S(1)} %collective-permute-done.3.refs_3_, ...), custom_call_target="tpu_custom_call" | custom-call | tf_op jit(solution)/shard_map/pallas_call | solution.py:55
  89.8 14.1 %all-to-all-start = ((bf16[64,24,320]{2,1,0:T(8,128)(2,1)}), bf16[64,24,320]{2,1,0:T(8,128)(2,1)}, u32[]{:S(2)}, u32[]{:S(2)}) async-start(bf16[64,24,320]{2,1,0:T(8,128)(2,1)} %copy-done.1), calls=%async_computation | async-start | bytes 2359296 | tf_op jit(solution)/shard_map/all_to_all | solution.py:240
  105.6 29.7 %all-to-all-done.arrived = bf16[64,24,320]{2,1,0:T(8,128)(2,1)} async-done(((bf16[64,24,320]{2,1,0:T(8,128)(2,1)}), bf16[64,24,320]{2,1,0:T(8,128)(2,1)}, u32[]{:S(2)}, u32[]{:S(2)}) %all-to-all-start) | async-done | bytes 983072 | tf_op jit(solution)/shard_map/all_to_all | solution.py:240
  140.1 4.7 %shard_map.132 = (bf16[4,96,1280]{2,1,0:T(8,128)(2,1)S(1)}, bf16[4,96,1280]{2,1,0:T(8,128)(2,1)}) custom-call(bf16[96,320]{1,0:T(8,128)(2,1)S(1)} %get-tuple-element.24.kept, bf16[96,320]{1,0:T(8,128)(2,1)S(1)} %collective-permute-done.6.received, f32[192,320]{1,0:T(8,128)S(1)} %fusion.15.slope, bf16[5120,320]{1,0:T(8,128)(2,1)} %all-gather.4.cloned.1.call-done.table), custom_call_target="tpu_custom_call" | custom-call | tf_op jit(solution)/shard_map/pallas_call | solution.py:102
  144.8 2.1 collective-permute-start.7
  149.5 2.4 add_convert_fusion
  151.9 4.3 %all-to-all-start.1 = ((bf16[4,96,1280]{2,1,0:T(8,128)(2,1)}), bf16[4,96,1280]{2,1,0:T(8,128)(2,1)S(1)}, u32[]{:S(2)}, u32[]{:S(2)}) async-start(bf16[4,96,1280]{2,1,0:T(8,128)(2,1)} %add_convert_fusion), calls=%async_computation.1 | async-start | bytes 1966080 | tf_op jit(solution)/shard_map/all_to_all | solution.py:253
  156.8 14.3 %all-to-all-done.1.parts = bf16[4,96,1280]{2,1,0:T(8,128)(2,1)S(1)} async-done(((bf16[4,96,1280]{2,1,0:T(8,128)(2,1)}), bf16[4,96,1280]{2,1,0:T(8,128)(2,1)S(1)}, u32[]{:S(2)}, u32[]{:S(2)}) %all-to-all-start.1) | async-done | bytes 983072 | tf_op jit(solution)/shard_map/all_to_all | solution.py:253
  171.6 15.0 %all_gather.18.near = bf16[384,1280]{1,0:T(8,128)(2,1)S(1)} all-gather(bf16[96,1280]{1,0:T(8,128)(2,1)S(1)} %shard_map.133), channel_id=1, replica_groups=mesh['gx'=4,'gc'=2,'z'=8,'y'=8] {'gx'}, dimensions={0}, use_global_device_ids=true | all-gather | bytes 1228800 | tf_op jit(solution)/shard_map/all_gather | solution.py:284
  186.6 2.1 collective-permute-start.8
  188.9 2.9 %multiply_convert_fusion = (bf16[768,320]{1,0:T(8,128)(2,1)S(1)}, f32[768,320]{1,0:T(8,128)}) fusion(bf16[768,1,320]{0,2,1:T(8,128)(2,1)} %param.17, s32[768]{0:T(1024)S(1)} %constant_dynamic-update-slice_fusion.3), kind=kOutput, calls=%fused_computation.13 | convolution fusion | flops 379551744 | bytes 1969152 | tf_op jit(solution)/shard_map/dot_general | solution.py:278
  191.9 2.9 %shard_map.134 = bf16[64,56,128]{2,1,0:T(8,128)(2,1)S(1)} custom-call(bf16[384,1280]{1,0:T(8,128)(2,1)S(1)} %all_gather.18.near, bf16[384,1280]{1,0:T(8,128)(2,1)} %collective-permute-done.8.far, bf16[768,320]{1,0:T(8,128)(2,1)S(1)} %get-tuple-element.41.activation), custom_call_target="tpu_custom_call" | custom-call | tf_op jit(solution)/shard_map/pallas_call | solution.py:157
  195.7 7.0 %all-to-all-start.2 = ((bf16[64,56,128]{2,1,0:T(8,128)(2,1)}), bf16[64,56,128]{2,1,0:T(8,128)(2,1)}, u32[]{:S(2)}, u32[]{:S(2)}) async-start(bf16[64,56,128]{2,1,0:T(8,128)(2,1)} %copy-done.2), calls=%async_computation.2 | async-start | bytes 1835008 | tf_op jit(solution)/shard_map/all_to_all | solution.py:288
  202.7 2.4 %slice.37 = bf16[64,20,320]{2,1,0:T(8,128)(2,1)} slice(bf16[64,32,320]{2,1,0:T(8,128)(2,1)} %bitcast.66), slice={[0:64], [0:20], [0:320]} | slice | bytes 1638400 | tf_op jit(solution)/shard_map/slice | solution.py:292
  205.1 2.3 reshape.411
  211.2 4.6 %fusion.6 = bf16[768,1,320]{0,2,1:T(8,128)(2,1)} fusion(s32[768]{0:T(1024)S(1)} %constant_dynamic-update-slice_fusion.3, bf16[768,1280]{1,0:T(8,128)(2,1)} %copy-done.7, bf16[1280,320]{1,0:T(8,128)(2,1)S(1)} %copy-done.8, f32[768,320]{1,0:T(8,128)} %get-tuple-element.42), kind=kOutput, calls=%fused_computation.12 | convolution fusion | flops 1009926144 | bytes 4262912 | tf_op jit(solution)/shard_map/dot_general | solution.py:295
  215.9 13.8 %all-to-all-done.2.arrived = bf16[64,56,128]{2,1,0:T(8,128)(2,1)} async-done(((bf16[64,56,128]{2,1,0:T(8,128)(2,1)}), bf16[64,56,128]{2,1,0:T(8,128)(2,1)}, u32[]{:S(2)}, u32[]{:S(2)}) %all-to-all-start.2) | async-done | bytes 917536 | tf_op jit(solution)/shard_map/all_to_all | solution.py:288
  (122 shorter events, 34.0 us)
Async XLA Ops:
  7.2 149.2 %copy-start = (bf16[768,1,1280]{2,0,1:T(8,128)(2,1)S(1)}, bf16[768,1,1280]{2,0,1:T(8,128)(2,1)}, u32[]{:S(2)}) copy-start(bf16[768,1,1280]{2,0,1:T(8,128)(2,1)} %param.16) | copy-start | bytes 5898244
  7.2 7.9 %copy-start.10 = (bf16[128,320]{0,1:T(8,128)(2,1)S(1)}, bf16[128,320]{0,1:T(8,128)(2,1)}, u32[]{:S(2)}) copy-start(bf16[128,320]{0,1:T(8,128)(2,1)} %param.19) | copy-start | bytes 245764
  7.2 132.9 %all-gather.4.cloned.1.call-start = ((), (), s32[]{:S(2)}) async-start(), calls=%async_computation.3 | async-start | bytes 3993600 | tf_op jit(solution)/shard_map/all_gather | solution.py:246
  13.4 31.6 %collective-permute-start = (bf16[192,1024]{1,0:T(8,128)(2,1)}, bf16[192,1024]{1,0:T(8,128)(2,1)S(1)}, u32[]{:S(2)}, u32[]{:S(2)}) collective-permute-start(bf16[192,1024]{1,0:T(8,128)(2,1)} %convolution_convert_fusion.2), channel_id=1, source_target_pairs={{0,0},{8,64},{16,128},{24,192},{32,256},{40,320},{48,384},{56,448}... | collective-permute-start | bytes 1179656 | tf_op jit(solution)/shard_map/ppermute | solution.py:225
  45.7 37.2 %collective-permute-start.5 = (bf16[8,160,320]{2,1,0:T(8,128)(2,1)S(1)}, bf16[8,160,320]{2,1,0:T(8,128)(2,1)}, u32[]{:S(2)}, u32[]{:S(2)}) collective-permute-start(bf16[8,160,320]{2,1,0:T(8,128)(2,1)S(1)} %bitcast.63), channel_id=1, source_target_pairs={{0,64},{64,0},{1,65},{65,1},{2,66},{66,2},{3,67},{67,3},{4,68},{68... | collective-permute-start | bytes 2457608 | tf_op jit(solution)/shard_map/ppermute | solution.py:23
  47.6 21.8 %collective-permute-start.1 = (bf16[192,1024]{1,0:T(8,128)(2,1)}, bf16[192,1024]{1,0:T(8,128)(2,1)S(1)}, u32[]{:S(2)}, u32[]{:S(2)}) collective-permute-start(bf16[192,1024]{1,0:T(8,128)(2,1)} %copy-done.5), channel_id=1, source_target_pairs={{0,128},{128,256},{256,384},{384,0},{1,129},{129,257},{257,385},{3... | collective-permute-start | bytes 1179656 | tf_op jit(solution)/shard_map/ppermute | solution.py:23
  53.8 18.3 %collective-permute-start.2 = (bf16[192,1024]{1,0:T(8,128)(2,1)}, bf16[192,1024]{1,0:T(8,128)(2,1)S(1)}, u32[]{:S(2)}, u32[]{:S(2)}) collective-permute-start(bf16[192,1024]{1,0:T(8,128)(2,1)} %copy-done.5), channel_id=1, source_target_pairs={{0,384},{128,0},{256,128},{384,256},{1,385},{129,1},{257,129},{385... | collective-permute-start | bytes 1179656 | tf_op jit(solution)/shard_map/ppermute | solution.py:23
  70.2 10.0 %collective-permute-start.3 = (bf16[96,1024]{1,0:T(8,128)(2,1)}, bf16[96,1024]{1,0:T(8,128)(2,1)S(1)}, u32[]{:S(2)}, u32[]{:S(2)}) collective-permute-start(bf16[96,1024]{1,0:T(8,128)(2,1)} %slice.33), channel_id=1, source_target_pairs={{0,128},{128,256},{256,384},{384,0},{1,129},{129,257},{257,385},{3... | collective-permute-start | bytes 589832 | tf_op jit(solution)/shard_map/ppermute | solution.py:23
  73.6 9.4 %collective-permute-start.4 = (bf16[96,1024]{1,0:T(8,128)(2,1)}, bf16[96,1024]{1,0:T(8,128)(2,1)}, u32[]{:S(2)}, u32[]{:S(2)}) collective-permute-start(bf16[96,1024]{1,0:T(8,128)(2,1)} %slice.34), channel_id=1, source_target_pairs={{0,384},{128,0},{256,128},{384,256},{1,385},{129,1},{257,129},{385... | collective-permute-start | bytes 589832 | tf_op jit(solution)/shard_map/ppermute | solution.py:23
  82.9 1.0 copy-start.4
  88.8 1.0 copy-start.1
  89.8 14.6 %copy-start.13 = (f32[1280]{0:T(1024)S(1)}, f32[1280]{0:T(1024)}, u32[]{:S(2)}) copy-start(f32[1280]{0:T(1024)} %param.18) | copy-start | bytes 15364
  89.8 15.4 %copy-start.9 = (bf16[192,1,320]{2,0,1:T(8,128)(2,1)S(1)}, bf16[192,1,320]{2,0,1:T(8,128)(2,1)}, u32[]{:S(2)}) copy-start(bf16[192,1,320]{2,0,1:T(8,128)(2,1)} %param.15) | copy-start | bytes 368644
  89.8 45.5 %all-to-all-start = ((bf16[64,24,320]{2,1,0:T(8,128)(2,1)}), bf16[64,24,320]{2,1,0:T(8,128)(2,1)}, u32[]{:S(2)}, u32[]{:S(2)}) async-start(bf16[64,24,320]{2,1,0:T(8,128)(2,1)} %copy-done.1), calls=%async_computation | async-start | bytes 2359296 | tf_op jit(solution)/shard_map/all_to_all | solution.py:240
  103.9 98.8 %all-gather.6.cloned.1.call-start = ((), (), s32[]{:S(2)}) async-start(), calls=%async_computation.4 | async-start | bytes 1769472 | tf_op jit(solution)/shard_map/all_gather | solution.py:248
  105.4 33.4 %copy-start.12 = (s32[4096]{0:T(1024)S(1)}, s32[4096]{0:T(1024)}, u32[]{:S(2)}) copy-start(s32[4096]{0:T(1024)} %param.13) | copy-start | bytes 49156
  105.4 33.5 %copy-start.11 = (s32[4096,2]{0,1:T(2,128)S(1)}, s32[4096,2]{0,1:T(2,128)}, u32[]{:S(2)}) copy-start(s32[4096,2]{0,1:T(2,128)} %param.12) | copy-start | bytes 98308
  136.9 3.2 %collective-permute-start.6 = (bf16[96,320]{1,0:T(8,128)(2,1)S(1)}, bf16[96,320]{1,0:T(8,128)(2,1)S(1)}, u32[]{:S(2)}, u32[]{:S(2)}) collective-permute-start(bf16[96,320]{1,0:T(8,128)(2,1)S(1)} %get-tuple-element.25), channel_id=1, source_target_pairs={{0,64},{64,0},{1,65},{65,1},{2,66},{66,2},{3,67},{67,3},{4,68},{68... | collective-permute-start | bytes 184328 | tf_op jit(solution)/shard_map/ppermute | solution.py:23
  144.8 4.8 %collective-permute-start.7 = (bf16[4,96,1280]{2,1,0:T(8,128)(2,1)}, bf16[4,96,1280]{2,1,0:T(8,128)(2,1)}, u32[]{:S(2)}, u32[]{:S(2)}) collective-permute-start(bf16[4,96,1280]{2,1,0:T(8,128)(2,1)} %get-tuple-element.28), channel_id=1, source_target_pairs={{0,64},{64,0},{1,65},{65,1},{2,66},{66,2},{3,67},{67,3},{4,68},{68... | collective-permute-start | bytes 2949128 | tf_op jit(solution)/shard_map/ppermute | solution.py:23
  151.9 19.2 %all-to-all-start.1 = ((bf16[4,96,1280]{2,1,0:T(8,128)(2,1)}), bf16[4,96,1280]{2,1,0:T(8,128)(2,1)S(1)}, u32[]{:S(2)}, u32[]{:S(2)}) async-start(bf16[4,96,1280]{2,1,0:T(8,128)(2,1)} %add_convert_fusion), calls=%async_computation.1 | async-start | bytes 1966080 | tf_op jit(solution)/shard_map/all_to_all | solution.py:253
  186.6 5.2 %collective-permute-start.8 = (bf16[384,1280]{1,0:T(8,128)(2,1)S(1)}, bf16[384,1280]{1,0:T(8,128)(2,1)}, u32[]{:S(2)}, u32[]{:S(2)}) collective-permute-start(bf16[384,1280]{1,0:T(8,128)(2,1)S(1)} %all_gather.18.near), channel_id=1, source_target_pairs={{0,64},{64,0},{1,65},{65,1},{2,66},{66,2},{3,67},{67,3},{4,68},{68... | collective-permute-start | bytes 2949128 | tf_op jit(solution)/shard_map/ppermute | solution.py:23
  195.7 34.0 %all-to-all-start.2 = ((bf16[64,56,128]{2,1,0:T(8,128)(2,1)}), bf16[64,56,128]{2,1,0:T(8,128)(2,1)}, u32[]{:S(2)}, u32[]{:S(2)}) async-start(bf16[64,56,128]{2,1,0:T(8,128)(2,1)} %copy-done.2), calls=%async_computation.2 | async-start | bytes 1835008 | tf_op jit(solution)/shard_map/all_to_all | solution.py:288
  208.7 1.3 copy-start.7
  210.0 1.2 copy-start.8
  (4 other events, 3.4 us)
Sparse Core Ops, SparseCore 0:
  11.0 101.5 all-gather.3
  115.3 55.0 all-gather.5

commit v3 on v2

--- a/solution.py
+++ b/solution.py
@@ -31,14 +31,14 @@
 
 
 def hidden_kernel(order, *refs):
-    pieces, (near, far, out, sums, table) = refs[:5], refs[5:]
-    last = jnp.concatenate([pieces[3][...], pieces[4][...]], axis=0)
+    pieces, (near, far, out, sums, table) = refs[:8], refs[8:]
+    table[:, 256:384] = jnp.zeros((1024, 128), BF16)
     for core, weight in enumerate((near, far)):
         for k in range(8):
-            table[k * 128 : (k + 1) * 128, :] = weight[k, 0:128, :]
+            table[k * 128 : (k + 1) * 128, 0:320] = weight[k, 0:128, :]
         w = table[...]
         for place in range(4):
-            rows = pieces[place][...] if place < 3 else last
+            rows = jnp.concatenate([half[...] for half in pieces[2 * place : 2 * place + 2]], axis=0)
             sums[order[place] + 4 * core] = jnp.dot(rows, w, preferred_element_type=F32)
     row = lax.broadcasted_iota(jnp.int32, (192, 192), 0)
     col = lax.broadcasted_iota(jnp.int32, (192, 192), 1)
@@ -47,17 +47,28 @@
     for part in range(8):
         block = sums[:, part * 24 : (part + 1) * 24, :].reshape(192, -1).astype(BF16)
         turned = jnp.dot(turn, block, preferred_element_type=F32)
-        out[part * 8 : (part + 1) * 8] = turned.reshape(8, 24, -1).astype(BF16)
+        last = turned[:, 256:384]
+        shifted_last = pltpu.roll(last, 64, 1).reshape(8, 24, 128)
+        last = last.reshape(8, 24, 128)
+        packed = jnp.concatenate(
+            [
+                turned[:, 0:128].reshape(8, 24, 128),
+                turned[:, 128:256].reshape(8, 24, 128),
+                last[:, 0:8] + shifted_last[:, 8:16],
+                last[:, 16:24],
+            ],
+            axis=1,
+        )
+        out[part * 8 : (part + 1) * 8] = packed.astype(BF16)
 
 
 def hidden_products(order, pieces, near, far):
-    width = near.shape[2]
     return pl.pallas_call(
         hidden_kernel,
-        out_shape=jax.ShapeDtypeStruct((64, 24, width), BF16),
-        in_specs=[whole(pltpu.SMEM)] + [whole()] * 7,
+        out_shape=jax.ShapeDtypeStruct((64, 64, 128), BF16),
+        in_specs=[whole(pltpu.SMEM)] + [whole()] * 10,
         out_specs=whole(),
-        scratch_shapes=[pltpu.VMEM((8, 192, width), F32), pltpu.VMEM((1024, width), BF16)],
+        scratch_shapes=[pltpu.VMEM((8, 192, 384), F32), pltpu.VMEM((1024, 384), BF16)],
         compiler_params=PARAMS,
     )(order, *pieces, near, far)
 
@@ -66,17 +77,22 @@
     total = arrived[0:8].astype(F32)
     for k in range(1, 8):
         total = total + arrived[8 * k : 8 * k + 8].astype(F32)
-    hidden = total.reshape(192, -1).astype(BF16)
+    last = total[:, 48:56]
+    second = pltpu.roll(last.reshape(64, 128), 64, 1).reshape(8, 8, 128)
+    last = jnp.concatenate([last, second, total[:, 56:64]], axis=1)
+    hidden = jnp.concatenate(
+        [part.reshape(192, 128) for part in (total[:, 0:24], total[:, 24:48], last)], axis=1
+    ).astype(BF16)
     row = lax.broadcasted_iota(jnp.int32, (96, 192), 0)
     col = lax.broadcasted_iota(jnp.int32, (96, 192), 1)
     first = row // 12 * 24 + row % 12
     for half, out in enumerate((keep, send)):
         pick = jnp.where(first + 12 * half == col, 1.0, 0.0).astype(BF16)
-        out[...] = jnp.dot(pick, hidden, preferred_element_type=F32).astype(BF16)
+        out[...] = jnp.dot(pick, hidden, preferred_element_type=F32)[:, 0:320].astype(BF16)
 
 
 def hidden_sums(arrived):
-    half = jax.ShapeDtypeStruct((96, arrived.shape[2]), BF16)
+    half = jax.ShapeDtypeStruct((96, 320), BF16)
     return pl.pallas_call(
         sum_kernel,
         out_shape=(half, half),
@@ -227,11 +243,14 @@
     )
     turned, along_y = lax.optimization_barrier((turned, along_y))
     across = shifted(along_y, "gc", 1)
-    left = shifted(turned, "gx", 1)
-    right = shifted(turned, "gx", -1)
-    far_a = shifted(left[:96], "gx", 1)
-    far_b = shifted(right[96:], "gx", -1)
-    pieces = [turned, left, right, far_a, far_b]
+    top, low = turned[:96], turned[96:]
+    left_top = shifted(top, "gx", 1)
+    right_low = shifted(low, "gx", -1)
+    left_low = shifted(low, "gx", 1)
+    right_top = shifted(top, "gx", -1)
+    far_top = shifted(left_top, "gx", 1)
+    far_low = shifted(right_low, "gx", -1)
+    pieces = [top, low, left_top, left_low, right_top, right_low, far_top, far_low]
     order = jnp.stack([(x + step) % 4 for step in (0, 3, 1, 2)]).astype(jnp.int32)
     partial = hidden_products(order, pieces, along_y, across)
     partial, merger_pre, image_owner, image_grid, vit_pre, vit_out = lax.optimization_barrier(
@@ -245,20 +264,20 @@
     slope = gelu_slope(pre_act.astype(F32))
     table = lax.all_gather(merger_in_w.T, SEQ, axis=0, tiled=True)
     fc2_y = along_y[:, 128:, :].reshape(256, -1)
+    arrived, fc2_y = lax.optimization_barrier((arrived, fc2_y))
     fc2 = lax.all_gather(fc2_y, "z", axis=0, tiled=True)
     kept, passed = hidden_sums(arrived)
     own, other = merged_products(kept, shifted(passed, "gc", 1), slope, table)
-    swapped = shifted(other, "gc", 1)
-    pair = (own.astype(F32) + swapped.astype(F32)).astype(BF16)
+    pair = (own.astype(F32) + shifted(other, "gc", 1).astype(F32)).astype(BF16)
     parts = lax.all_to_all(pair, "gx", split_axis=0, concat_axis=0, tiled=True)
 
     grids = image_grid.reshape(64, 64, 2)
     counts = grids[:, :, 0] * grids[:, :, 1]
     widths = grids[:, :, 1]
     owners = image_owner.reshape(64, 64)
-    received = (owners == own_index).astype(jnp.int32)
-    recv_counts = jnp.sum(received * counts, 1)
-    recv_widths = jnp.sum(received * widths, 1)
+    taken = (owners == own_index).astype(jnp.int32)
+    recv_counts = jnp.sum(taken * counts, 1)
+    recv_widths = jnp.sum(taken * widths, 1)
     j = jnp.arange(SLOT, dtype=jnp.int32)[None, :]
     w = recv_widths[:, None]
     base = peers[:, None] * (4 * SLOT) + (2 * (j // w)) * (2 * w) + 2 * (j % w)

time: 240 us -> 236 us (0.983)
  waiting for transfers between devices: 71.7 us -> 61.3 us
  starting transfers between devices: 55.9 us -> 63.6 us
    ppermute x8 -> x10, waiting for transfers between devices: 13.2 us -> 4.91 us  [shifted(): lax.ppermute(value, axis, [(i, (i + step) % size) for i in range(size)])]
    ppermute x8 -> x10, starting transfers between devices: 28.8 us -> 35.9 us  [shifted(): lax.ppermute(value, axis, [(i, (i + step) % size) for i in range(size)])]
    unnamed x31 -> x23, local copies, waits for them, and re-layouts: 6.95 us -> 5.11 us
  transfers between devices with their start and end apart: 14 -> 16, of which waited for: 7 -> 6; matrix products, arithmetic and copies ran while one was open for 12% -> 12% of each run, Pallas kernels for 6% -> 4%
where the time goes in v3:
time: 236 us; the launch traced here: 235 us
  starting transfers between devices  63.6 us (27%)
  waiting for transfers between devices  61.3 us (26%)
  blocking collectives  44.3 us (19%)
  local copies, waits for them, and re-layouts  19.3 us (8%)
  between operations  16 us (7%)
  Pallas kernels  15.7 us (7%)
  matrix products  11.3 us (5%)
  other arithmetic  3.29 us (1%)
    ppermute x10, starting transfers between devices, shifted(): lax.ppermute(value, axis, [(i, (i + step) % size) for i in range(size)])  35.9 us
    all_gather x1, blocking collectives, on_device(): lax.all_gather(jnp.concatenate([merger_out_w, fc2_rows], axis=0), 'y', ax...  29.5 us
    all_to_all x1, waiting for transfers between devices, on_device(): lax.all_to_all(partial, SEQ, split_axis=0, concat_axis=0, tiled=True)  27.6 us
    all_gather x1, blocking collectives, on_device(): near_grad = lax.all_gather(grad, 'gx', axis=0, tiled=True)  14.8 us
    all_to_all x1, waiting for transfers between devices, on_device(): lax.all_to_all(sent, SEQ, split_axis=0, concat_axis=0, tiled=True)  13.8 us
    all_to_all x1, waiting for transfers between devices, on_device(): parts = lax.all_to_all(pair, 'gx', split_axis=0, concat_axis=0, tiled=True)  13.8 us
    all_to_all x1, starting transfers between devices, on_device(): lax.all_to_all(partial, SEQ, split_axis=0, concat_axis=0, tiled=True)  13.6 us
    all_to_all x1, starting transfers between devices, on_device(): lax.all_to_all(sent, SEQ, split_axis=0, concat_axis=0, tiled=True)  7.84 us
  transfers between devices with their start and end apart: 16, of which 6 were waited for; matrix products, arithmetic and copies ran while one was open for 12% of the time, Pallas kernels for 4%

profile of v3, /device:TPU:8, one launch (start us, length us, event | category | flops | bytes accessed | tf_op | source)
XLA Modules:
  0.0 234.8 jit_solution(15930387410978947787)
XLA Ops:
  12.1 2.1 convolution_convert_fusion.2
  16.9 29.5 %all-gather = bf16[1280,320]{1,0:T(8,128)(2,1)S(1)} all-gather(bf16[160,320]{1,0:T(8,128)(2,1)S(1)} %pad_maximum_fusion), channel_id=2, replica_groups=mesh['gx'=4,'gc'=2,'z'=8,'y'=8] {'y'}, dimensions={0}, use_global_device_ids=true | all-gather | bytes 921600 | tf_op jit(solution)/shard_map/all_gather | solution.py:240
  50.1 5.8 %collective-permute-start.1 = (bf16[96,1024]{1,0:T(8,128)(2,1)S(1)}, bf16[96,1024]{1,0:T(8,128)(2,1)S(1)}, u32[]{:S(2)}, u32[]{:S(2)}) collective-permute-start(bf16[96,1024]{1,0:T(8,128)(2,1)S(1)} %get-tuple-element.40.refs_0_), channel_id=1, source_target_pairs={{0,128},{128,256},{256,384},{384,0},{1,129},{129,257},{257,385},{3... | collective-permute-start | bytes 589832 | tf_op jit(solution)/shard_map/ppermute | solution.py:23
  55.9 8.1 %collective-permute-start.4 = (bf16[96,1024]{1,0:T(8,128)(2,1)S(1)}, bf16[96,1024]{1,0:T(8,128)(2,1)}, u32[]{:S(2)}, u32[]{:S(2)}) collective-permute-start(bf16[96,1024]{1,0:T(8,128)(2,1)S(1)} %get-tuple-element.39.refs_1_), channel_id=1, source_target_pairs={{0,384},{128,0},{256,128},{384,256},{1,385},{129,1},{257,129},{385... | collective-permute-start | bytes 589832 | tf_op jit(solution)/shard_map/ppermute | solution.py:23
  66.0 5.1 %collective-permute-start.3 = (bf16[96,1024]{1,0:T(8,128)(2,1)S(1)}, bf16[96,1024]{1,0:T(8,128)(2,1)}, u32[]{:S(2)}, u32[]{:S(2)}) collective-permute-start(bf16[96,1024]{1,0:T(8,128)(2,1)S(1)} %get-tuple-element.40.refs_0_), channel_id=1, source_target_pairs={{0,384},{128,0},{256,128},{384,256},{1,385},{129,1},{257,129},{385... | collective-permute-start | bytes 589832 | tf_op jit(solution)/shard_map/ppermute | solution.py:23
  73.0 5.1 %collective-permute-start.6 = (bf16[96,1024]{1,0:T(8,128)(2,1)}, bf16[96,1024]{1,0:T(8,128)(2,1)}, u32[]{:S(2)}, u32[]{:S(2)}) collective-permute-start(bf16[96,1024]{1,0:T(8,128)(2,1)} %collective-permute-done.4.refs_5_), channel_id=1, source_target_pairs={{0,384},{128,0},{256,128},{384,256},{1,385},{129,1},{257,129},{385... | collective-permute-start | bytes 589832 | tf_op jit(solution)/shard_map/ppermute | solution.py:23
  78.3 2.5 %collective-permute-done.5.refs_6_ = bf16[96,1024]{1,0:T(8,128)(2,1)} collective-permute-done((bf16[96,1024]{1,0:T(8,128)(2,1)S(1)}, bf16[96,1024]{1,0:T(8,128)(2,1)}, u32[]{:S(2)}, u32[]{:S(2)}) %collective-permute-start.5) | collective-permute-done | bytes 196640 | tf_op jit(solution)/shard_map/ppermute | solution.py:23
  82.1 4.2 %shard_map.130 = bf16[64,64,128]{2,1,0:T(8,128)(2,1)S(1)} custom-call(s32[4]{0:T(128)S(1)} %pad_add_fusion.order, bf16[96,1024]{1,0:T(8,128)(2,1)S(1)} %get-tuple-element.40.refs_0_, bf16[96,1024]{1,0:T(8,128)(2,1)S(1)} %get-tuple-element.39.refs_1_, bf16[96,1024]{1,0:T(8,128)(2,1)S(1)} %collective-permute-done.1.refs_2_, ...), custom_call_target="tpu_custom_call" | custom-call | tf_op jit(solution)/shard_map/pallas_call | solution.py:66
  87.4 13.6 %all-to-all-start = ((bf16[64,64,128]{2,1,0:T(8,128)(2,1)}), bf16[64,64,128]{2,1,0:T(8,128)(2,1)}, u32[]{:S(2)}, u32[]{:S(2)}) async-start(bf16[64,64,128]{2,1,0:T(8,128)(2,1)} %copy-done.1), calls=%async_computation | async-start | bytes 2097152 | tf_op jit(solution)/shard_map/all_to_all | solution.py:259
  102.7 27.6 %all-to-all-done.arrived = bf16[64,64,128]{2,1,0:T(8,128)(2,1)} async-done(((bf16[64,64,128]{2,1,0:T(8,128)(2,1)}), bf16[64,64,128]{2,1,0:T(8,128)(2,1)}, u32[]{:S(2)}, u32[]{:S(2)}) %all-to-all-start) | async-done | bytes 1048608 | tf_op jit(solution)/shard_map/all_to_all | solution.py:259
  135.0 4.6 %shard_map.132 = (bf16[4,96,1280]{2,1,0:T(8,128)(2,1)S(1)}, bf16[4,96,1280]{2,1,0:T(8,128)(2,1)}) custom-call(bf16[96,320]{1,0:T(8,128)(2,1)S(1)} %get-tuple-element.27.kept, bf16[96,320]{1,0:T(8,128)(2,1)S(1)} %collective-permute-done.8.received, f32[192,320]{1,0:T(8,128)S(1)} %fusion.15.slope, bf16[5120,320]{1,0:T(8,128)(2,1)} %all-gather.4.cloned.1.call-done.table), custom_call_target="tpu_custom_call" | custom-call | tf_op jit(solution)/shard_map/pallas_call | solution.py:118
  139.6 2.1 collective-permute-start.9
  144.4 2.4 %add_convert_fusion = bf16[4,96,1280]{2,1,0:T(8,128)(2,1)} fusion(bf16[4,96,1280]{2,1,0:T(8,128)(2,1)} %collective-permute-done.9, bf16[4,96,1280]{2,1,0:T(8,128)(2,1)S(1)} %get-tuple-element.30), kind=kLoop, calls=%fused_computation.7 | loop fusion | flops 1966080 | bytes 2949120 | tf_op jit(solution)/shard_map/convert_element_type | solution.py:271
  146.7 4.5 %all-to-all-start.1 = ((bf16[4,96,1280]{2,1,0:T(8,128)(2,1)}), bf16[4,96,1280]{2,1,0:T(8,128)(2,1)S(1)}, u32[]{:S(2)}, u32[]{:S(2)}) async-start(bf16[4,96,1280]{2,1,0:T(8,128)(2,1)} %add_convert_fusion), calls=%async_computation.1 | async-start | bytes 1966080 | tf_op jit(solution)/shard_map/all_to_all | solution.py:272
  152.4 13.8 %all-to-all-done.1.parts = bf16[4,96,1280]{2,1,0:T(8,128)(2,1)S(1)} async-done(((bf16[4,96,1280]{2,1,0:T(8,128)(2,1)}), bf16[4,96,1280]{2,1,0:T(8,128)(2,1)S(1)}, u32[]{:S(2)}, u32[]{:S(2)}) %all-to-all-start.1) | async-done | bytes 983072 | tf_op jit(solution)/shard_map/all_to_all | solution.py:272
  166.6 14.8 %all_gather.18.near = bf16[384,1280]{1,0:T(8,128)(2,1)S(1)} all-gather(bf16[96,1280]{1,0:T(8,128)(2,1)S(1)} %shard_map.133), channel_id=1, replica_groups=mesh['gx'=4,'gc'=2,'z'=8,'y'=8] {'gx'}, dimensions={0}, use_global_device_ids=true | all-gather | bytes 1228800 | tf_op jit(solution)/shard_map/all_gather | solution.py:303
  181.4 2.1 collective-permute-start.10
  183.7 2.9 %multiply_convert_fusion = (bf16[768,320]{1,0:T(8,128)(2,1)S(1)}, f32[768,320]{1,0:T(8,128)}) fusion(bf16[768,1,320]{0,2,1:T(8,128)(2,1)} %param.17, s32[768]{0:T(1024)S(1)} %constant_dynamic-update-slice_fusion.3), kind=kOutput, calls=%fused_computation.13 | convolution fusion | flops 379551744 | bytes 1969152 | tf_op jit(solution)/shard_map/dot_general | solution.py:297
  186.7 2.9 %shard_map.134 = bf16[64,56,128]{2,1,0:T(8,128)(2,1)S(1)} custom-call(bf16[384,1280]{1,0:T(8,128)(2,1)S(1)} %all_gather.18.near, bf16[384,1280]{1,0:T(8,128)(2,1)} %collective-permute-done.10.far, bf16[768,320]{1,0:T(8,128)(2,1)S(1)} %get-tuple-element.47.activation), custom_call_target="tpu_custom_call" | custom-call | tf_op jit(solution)/shard_map/pallas_call | solution.py:173
  190.5 7.8 %all-to-all-start.2 = ((bf16[64,56,128]{2,1,0:T(8,128)(2,1)}), bf16[64,56,128]{2,1,0:T(8,128)(2,1)}, u32[]{:S(2)}, u32[]{:S(2)}) async-start(bf16[64,56,128]{2,1,0:T(8,128)(2,1)} %copy-done.2), calls=%async_computation.2 | async-start | bytes 1835008 | tf_op jit(solution)/shard_map/all_to_all | solution.py:307
  198.4 2.4 %slice.35 = bf16[64,20,320]{2,1,0:T(8,128)(2,1)} slice(bf16[64,32,320]{2,1,0:T(8,128)(2,1)} %bitcast.66), slice={[0:64], [0:20], [0:320]} | slice | bytes 1638400 | tf_op jit(solution)/shard_map/slice | solution.py:311
  200.9 2.3 reshape.411
  207.0 4.6 %fusion.6 = bf16[768,1,320]{0,2,1:T(8,128)(2,1)} fusion(s32[768]{0:T(1024)S(1)} %constant_dynamic-update-slice_fusion.3, bf16[768,1280]{1,0:T(8,128)(2,1)} %copy-done.3, bf16[1280,320]{1,0:T(8,128)(2,1)S(1)} %copy-done.4, f32[768,320]{1,0:T(8,128)} %get-tuple-element.48), kind=kOutput, calls=%fused_computation.12 | convolution fusion | flops 1009926144 | bytes 4262912 | tf_op jit(solution)/shard_map/dot_general | solution.py:314
  211.6 13.8 %all-to-all-done.2.arrived = bf16[64,56,128]{2,1,0:T(8,128)(2,1)} async-done(((bf16[64,56,128]{2,1,0:T(8,128)(2,1)}), bf16[64,56,128]{2,1,0:T(8,128)(2,1)}, u32[]{:S(2)}, u32[]{:S(2)}) %all-to-all-start.2) | async-done | bytes 917536 | tf_op jit(solution)/shard_map/all_to_all | solution.py:307
  (117 shorter events, 34.3 us)
Async XLA Ops:
  8.0 143.9 %copy-start = (bf16[768,1,1280]{2,0,1:T(8,128)(2,1)S(1)}, bf16[768,1,1280]{2,0,1:T(8,128)(2,1)}, u32[]{:S(2)}) copy-start(bf16[768,1,1280]{2,0,1:T(8,128)(2,1)} %param.16) | copy-start | bytes 5898244
  8.0 127.0 %all-gather.4.cloned.1.call-start = ((), (), s32[]{:S(2)}) async-start(), calls=%async_computation.3 | async-start | bytes 3993600 | tf_op jit(solution)/shard_map/all_gather | solution.py:265
  14.2 32.2 %collective-permute-start = (bf16[192,1024]{1,0:T(8,128)(2,1)}, bf16[192,1024]{1,0:T(8,128)(2,1)S(1)}, u32[]{:S(2)}, u32[]{:S(2)}) collective-permute-start(bf16[192,1024]{1,0:T(8,128)(2,1)} %convolution_convert_fusion.2), channel_id=1, source_target_pairs={{0,0},{8,64},{16,128},{24,192},{32,256},{40,320},{48,384},{56,448}... | collective-permute-start | bytes 1179656 | tf_op jit(solution)/shard_map/ppermute | solution.py:241
  47.1 35.0 %collective-permute-start.7 = (bf16[8,160,320]{2,1,0:T(8,128)(2,1)S(1)}, bf16[8,160,320]{2,1,0:T(8,128)(2,1)}, u32[]{:S(2)}, u32[]{:S(2)}) collective-permute-start(bf16[8,160,320]{2,1,0:T(8,128)(2,1)S(1)} %bitcast.63), channel_id=1, source_target_pairs={{0,64},{64,0},{1,65},{65,1},{2,66},{66,2},{3,67},{67,3},{4,68},{68... | collective-permute-start | bytes 2457608 | tf_op jit(solution)/shard_map/ppermute | solution.py:23
  50.1 20.9 %collective-permute-start.1 = (bf16[96,1024]{1,0:T(8,128)(2,1)S(1)}, bf16[96,1024]{1,0:T(8,128)(2,1)S(1)}, u32[]{:S(2)}, u32[]{:S(2)}) collective-permute-start(bf16[96,1024]{1,0:T(8,128)(2,1)S(1)} %get-tuple-element.40.refs_0_), channel_id=1, source_target_pairs={{0,128},{128,256},{256,384},{384,0},{1,129},{129,257},{257,385},{3... | collective-permute-start | bytes 589832 | tf_op jit(solution)/shard_map/ppermute | solution.py:23
  55.9 17.1 %collective-permute-start.4 = (bf16[96,1024]{1,0:T(8,128)(2,1)S(1)}, bf16[96,1024]{1,0:T(8,128)(2,1)}, u32[]{:S(2)}, u32[]{:S(2)}) collective-permute-start(bf16[96,1024]{1,0:T(8,128)(2,1)S(1)} %get-tuple-element.39.refs_1_), channel_id=1, source_target_pairs={{0,384},{128,0},{256,128},{384,256},{1,385},{129,1},{257,129},{385... | collective-permute-start | bytes 589832 | tf_op jit(solution)/shard_map/ppermute | solution.py:23
  64.0 14.3 %collective-permute-start.2 = (bf16[96,1024]{1,0:T(8,128)(2,1)S(1)}, bf16[96,1024]{1,0:T(8,128)(2,1)}, u32[]{:S(2)}, u32[]{:S(2)}) collective-permute-start(bf16[96,1024]{1,0:T(8,128)(2,1)S(1)} %get-tuple-element.39.refs_1_), channel_id=1, source_target_pairs={{0,128},{128,256},{256,384},{384,0},{1,129},{129,257},{257,385},{3... | collective-permute-start | bytes 589832 | tf_op jit(solution)/shard_map/ppermute | solution.py:23
  66.0 12.3 %collective-permute-start.3 = (bf16[96,1024]{1,0:T(8,128)(2,1)S(1)}, bf16[96,1024]{1,0:T(8,128)(2,1)}, u32[]{:S(2)}, u32[]{:S(2)}) collective-permute-start(bf16[96,1024]{1,0:T(8,128)(2,1)S(1)} %get-tuple-element.40.refs_0_), channel_id=1, source_target_pairs={{0,384},{128,0},{256,128},{384,256},{1,385},{129,1},{257,129},{385... | collective-permute-start | bytes 589832 | tf_op jit(solution)/shard_map/ppermute | solution.py:23
  71.1 9.7 %collective-permute-start.5 = (bf16[96,1024]{1,0:T(8,128)(2,1)S(1)}, bf16[96,1024]{1,0:T(8,128)(2,1)}, u32[]{:S(2)}, u32[]{:S(2)}) collective-permute-start(bf16[96,1024]{1,0:T(8,128)(2,1)S(1)} %collective-permute-done.1.refs_2_), channel_id=1, source_target_pairs={{0,128},{128,256},{256,384},{384,0},{1,129},{129,257},{257,385},{3... | collective-permute-start | bytes 589832 | tf_op jit(solution)/shard_map/ppermute | solution.py:23
  73.0 9.1 %collective-permute-start.6 = (bf16[96,1024]{1,0:T(8,128)(2,1)}, bf16[96,1024]{1,0:T(8,128)(2,1)}, u32[]{:S(2)}, u32[]{:S(2)}) collective-permute-start(bf16[96,1024]{1,0:T(8,128)(2,1)} %collective-permute-done.4.refs_5_), channel_id=1, source_target_pairs={{0,384},{128,0},{256,128},{384,256},{1,385},{129,1},{257,129},{385... | collective-permute-start | bytes 589832 | tf_op jit(solution)/shard_map/ppermute | solution.py:23
  86.3 1.0 copy-start.1
  87.4 14.1 %copy-start.9 = (f32[1280]{0:T(1024)S(1)}, f32[1280]{0:T(1024)}, u32[]{:S(2)}) copy-start(f32[1280]{0:T(1024)} %param.18) | copy-start | bytes 15364
  87.4 14.9 %copy-start.6 = (bf16[192,1,320]{2,0,1:T(8,128)(2,1)S(1)}, bf16[192,1,320]{2,0,1:T(8,128)(2,1)}, u32[]{:S(2)}) copy-start(bf16[192,1,320]{2,0,1:T(8,128)(2,1)} %param.15) | copy-start | bytes 368644
  87.4 42.9 %all-to-all-start = ((bf16[64,64,128]{2,1,0:T(8,128)(2,1)}), bf16[64,64,128]{2,1,0:T(8,128)(2,1)}, u32[]{:S(2)}, u32[]{:S(2)}) async-start(bf16[64,64,128]{2,1,0:T(8,128)(2,1)} %copy-done.1), calls=%async_computation | async-start | bytes 2097152 | tf_op jit(solution)/shard_map/all_to_all | solution.py:259
  101.5 32.2 %copy-start.8 = (s32[4096]{0:T(1024)S(1)}, s32[4096]{0:T(1024)}, u32[]{:S(2)}) copy-start(s32[4096]{0:T(1024)} %param.13) | copy-start | bytes 49156
  101.5 32.3 %copy-start.7 = (s32[4096,2]{0,1:T(2,128)S(1)}, s32[4096,2]{0,1:T(2,128)}, u32[]{:S(2)}) copy-start(s32[4096,2]{0,1:T(2,128)} %param.12) | copy-start | bytes 98308
  131.8 3.2 %collective-permute-start.8 = (bf16[96,320]{1,0:T(8,128)(2,1)S(1)}, bf16[96,320]{1,0:T(8,128)(2,1)S(1)}, u32[]{:S(2)}, u32[]{:S(2)}) collective-permute-start(bf16[96,320]{1,0:T(8,128)(2,1)S(1)} %get-tuple-element.28), channel_id=1, source_target_pairs={{0,64},{64,0},{1,65},{65,1},{2,66},{66,2},{3,67},{67,3},{4,68},{68... | collective-permute-start | bytes 184328 | tf_op jit(solution)/shard_map/ppermute | solution.py:23
  139.6 4.8 %collective-permute-start.9 = (bf16[4,96,1280]{2,1,0:T(8,128)(2,1)}, bf16[4,96,1280]{2,1,0:T(8,128)(2,1)}, u32[]{:S(2)}, u32[]{:S(2)}) collective-permute-start(bf16[4,96,1280]{2,1,0:T(8,128)(2,1)} %get-tuple-element.31), channel_id=1, source_target_pairs={{0,64},{64,0},{1,65},{65,1},{2,66},{66,2},{3,67},{67,3},{4,68},{68... | collective-permute-start | bytes 2949128 | tf_op jit(solution)/shard_map/ppermute | solution.py:23
  146.7 19.4 %all-to-all-start.1 = ((bf16[4,96,1280]{2,1,0:T(8,128)(2,1)}), bf16[4,96,1280]{2,1,0:T(8,128)(2,1)S(1)}, u32[]{:S(2)}, u32[]{:S(2)}) async-start(bf16[4,96,1280]{2,1,0:T(8,128)(2,1)} %add_convert_fusion), calls=%async_computation.1 | async-start | bytes 1966080 | tf_op jit(solution)/shard_map/all_to_all | solution.py:272
  151.3 47.1 %all-gather.6.cloned.1.call-start = ((), (), s32[]{:S(2)}) async-start(), calls=%async_computation.4 | async-start | bytes 1769472 | tf_op jit(solution)/shard_map/all_gather | solution.py:268
  181.4 5.2 %collective-permute-start.10 = (bf16[384,1280]{1,0:T(8,128)(2,1)S(1)}, bf16[384,1280]{1,0:T(8,128)(2,1)}, u32[]{:S(2)}, u32[]{:S(2)}) collective-permute-start(bf16[384,1280]{1,0:T(8,128)(2,1)S(1)} %all_gather.18.near), channel_id=1, source_target_pairs={{0,64},{64,0},{1,65},{65,1},{2,66},{66,2},{3,67},{67,3},{4,68},{68... | collective-permute-start | bytes 2949128 | tf_op jit(solution)/shard_map/ppermute | solution.py:23
  190.5 34.9 %all-to-all-start.2 = ((bf16[64,56,128]{2,1,0:T(8,128)(2,1)}), bf16[64,56,128]{2,1,0:T(8,128)(2,1)}, u32[]{:S(2)}, u32[]{:S(2)}) async-start(bf16[64,56,128]{2,1,0:T(8,128)(2,1)} %copy-done.2), calls=%async_computation.2 | async-start | bytes 1835008 | tf_op jit(solution)/shard_map/all_to_all | solution.py:307
  204.5 1.3 copy-start.3
  205.8 1.2 copy-start.4
  (2 other events, 1.7 us)
Sparse Core Ops, SparseCore 0:
  11.9 105.1 all-gather.3
Sparse Core Ops, SparseCore 1:
  154.4 39.4 all-gather.5

commit v4 on v3

--- a/solution.py
+++ b/solution.py
@@ -102,32 +102,32 @@
     )(arrived)
 
 
-def merged_kernel(kept, received, slope, table, own, other):
-    hidden = jnp.concatenate([kept[...], received[...]], axis=0).astype(F32)
-    grad = (slope[...] * hidden).astype(BF16)
+def merged_kernel(grads, table, own, other):
     dims = (((1,), (1,)), ((), ()))
-    for part in range(4):
-        w = table[part * 1280 : (part + 1) * 1280, :]
-        both = lax.dot_general(grad, w, dims, preferred_element_type=F32).astype(BF16)
-        own[part] = both[:96]
-        other[part] = both[96:]
-
-
-def merged_products(kept, received, slope, table):
-    half = jax.ShapeDtypeStruct((4, 96, 1280), BF16)
+    total = None
+    for k in range(4):
+        w = table[k * 1280 : (k + 1) * 1280, :]
+        part = lax.dot_general(grads[k], w, dims, preferred_element_type=F32)
+        total = part if total is None else total + part
+    own[...] = total[:96]
+    other[...] = total[96:].astype(BF16)
+
+
+def merged_products(grads, table):
     return pl.pallas_call(
         merged_kernel,
-        out_shape=(half, half),
-        in_specs=[whole()] * 4,
+        out_shape=(
+            jax.ShapeDtypeStruct((96, 1280), F32),
+            jax.ShapeDtypeStruct((96, 1280), BF16),
+        ),
+        in_specs=[whole()] * 2,
         out_specs=(whole(), whole()),
         compiler_params=PARAMS,
-    )(kept, received, slope, table)
-
-
-def norm_kernel(parts, inputs, gain, out):
-    upstream = parts[0].astype(F32)
-    for k in range(1, 4):
-        upstream = upstream + parts[k].astype(F32)
+    )(grads, table)
+
+
+def norm_kernel(own, swapped, inputs, gain, out):
+    upstream = own[...] + swapped[...].astype(F32)
     x = inputs[...].astype(F32)
     centred = x - jnp.mean(x, -1, keepdims=True)
     inverse_std = lax.rsqrt(jnp.mean(centred * centred, -1, keepdims=True) + 1e-06)
@@ -143,14 +143,14 @@
     ).astype(BF16)
 
 
-def norm_backward(parts, inputs, gain):
+def norm_backward(own, swapped, inputs, gain):
     return pl.pallas_call(
         norm_kernel,
         out_shape=jax.ShapeDtypeStruct((96, 1280), BF16),
-        in_specs=[whole()] * 3,
+        in_specs=[whole()] * 4,
         out_specs=whole(),
         compiler_params=PARAMS,
-    )(parts, inputs, gain)
+    )(own, swapped, inputs, gain)
 
 
 def weight_kernel(near, far, activation, out, total, turned, packed):
@@ -220,6 +220,17 @@
     x = lax.axis_index("gx")
     core = lax.axis_index("gc")
     own_index = lax.axis_index(SEQ)
+    in_w = lax.ppermute(
+        merger_in_w.T,
+        (*GRP, "z"),
+        [
+            ((2 * a + c) * 8 + z, (z // 2 * 2 + c) * 8 + 2 * a + z % 2)
+            for a in range(4)
+            for c in range(2)
+            for z in range(8)
+        ],
+    )
+
     peers = jnp.arange(64, dtype=jnp.int32)
     my_owners = lax.dynamic_slice_in_dim(image_owner, own_index * 64, 64)
     my_starts = lax.dynamic_slice_in_dim(row_start, own_index * 64, 64)
@@ -236,7 +247,8 @@
     rows = jnp.dot(pick, llm_grad, preferred_element_type=F32).astype(BF16)
 
     fc2_rows = jnp.pad(vit_fc2_w, ((0, 12), (0, 0)))
-    rows, fc2_rows = lax.optimization_barrier((rows, fc2_rows))
+    rows, fc2_rows, in_w = lax.optimization_barrier((rows, fc2_rows, in_w))
+    table = lax.all_gather(in_w, SEQ, axis=0, tiled=True)
     along_y = lax.all_gather(jnp.concatenate([merger_out_w, fc2_rows], axis=0), "y", axis=0)
     turned = lax.ppermute(
         rows, (*GRP, "z"), [(g * 8 + z, z * 8 + g) for g in range(8) for z in range(8)]
@@ -262,14 +274,14 @@
     pre_act = pre_act.reshape(2, 96, -1)
     pre_act = jnp.where(core == 0, pre_act, pre_act[::-1]).reshape(192, -1)
     slope = gelu_slope(pre_act.astype(F32))
-    table = lax.all_gather(merger_in_w.T, SEQ, axis=0, tiled=True)
     fc2_y = along_y[:, 128:, :].reshape(256, -1)
     arrived, fc2_y = lax.optimization_barrier((arrived, fc2_y))
     fc2 = lax.all_gather(fc2_y, "z", axis=0, tiled=True)
     kept, passed = hidden_sums(arrived)
-    own, other = merged_products(kept, shifted(passed, "gc", 1), slope, table)
-    pair = (own.astype(F32) + shifted(other, "gc", 1).astype(F32)).astype(BF16)
-    parts = lax.all_to_all(pair, "gx", split_axis=0, concat_axis=0, tiled=True)
+    hidden = jnp.concatenate([kept, shifted(passed, "gc", 1)], axis=0)
+    pre_grad = (slope * hidden.astype(F32)).astype(BF16)
+    own, other = merged_products(lax.all_gather(pre_grad, "gx", axis=0), table)
+    swapped = shifted(other, "gc", 1)
 
     grids = image_grid.reshape(64, 64, 2)
     counts = grids[:, :, 0] * grids[:, :, 1]
@@ -299,7 +311,7 @@
     activation = (fc_in * sigmoid_q).astype(BF16)
     fc_slope = sigmoid_q + 1.702 * fc_in * sigmoid_q * (1.0 - sigmoid_q)
 
-    grad = norm_backward(parts, norm_in, ln_gain.reshape(1, -1))
+    grad = norm_backward(own, swapped, norm_in, ln_gain.reshape(1, -1))
     near_grad = lax.all_gather(grad, "gx", axis=0, tiled=True)
     far_grad = shifted(near_grad, "gc", 1)
     sent = weight_products(near_grad, far_grad, activation)

time: 236 us -> 228 us (0.966)
  the two profiles are of different devices: /device:TPU:8 before, /device:TPU:2 now
where the time goes in v4:
time: 228 us; the launch traced here: 227 us
  starting transfers between devices  59.9 us (26%)
  blocking collectives  57.4 us (25%)
  waiting for transfers between devices  52.7 us (23%)
  local copies, waits for them, and re-layouts  19.5 us (9%)
  between operations  14.6 us (6%)
  Pallas kernels  12.1 us (5%)
  matrix products  9.58 us (4%)
    ppermute x10, starting transfers between devices, shifted(): lax.ppermute(value, axis, [(i, (i + step) % size) for i in range(size)])  32.6 us
    all_to_all x1, waiting for transfers between devices, on_device(): lax.all_to_all(partial, SEQ, split_axis=0, concat_axis=0, tiled=True)  28.9 us
    all_gather x1, blocking collectives, on_device(): lax.all_gather(jnp.concatenate([merger_out_w, fc2_rows], axis=0), 'y', ax...  28.3 us
    all_gather x1, blocking collectives, on_device(): near_grad = lax.all_gather(grad, 'gx', axis=0, tiled=True)  15.3 us
    all_gather x1, blocking collectives, on_device(): own, other = merged_products(lax.all_gather(pre_grad, 'gx', axis=0), table)  13.8 us
    all_to_all x1, waiting for transfers between devices, on_device(): lax.all_to_all(sent, SEQ, split_axis=0, concat_axis=0, tiled=True)  13.7 us
    all_to_all x1, starting transfers between devices, on_device(): lax.all_to_all(partial, SEQ, split_axis=0, concat_axis=0, tiled=True)  10.1 us
    ppermute x10, waiting for transfers between devices, shifted(): lax.ppermute(value, axis, [(i, (i + step) % size) for i in range(size)])  8.51 us
  transfers between devices with their start and end apart: 16, of which 9 were waited for; matrix products, arithmetic and copies ran while one was open for 11% of the time, Pallas kernels for 4%

profile of v4, /device:TPU:2, one launch (start us, length us, event | category | flops | bytes accessed | tf_op | source)
XLA Modules:
  0.0 226.8 jit_solution(2051908093470434936)
XLA Ops:
  7.2 6.2 %collective-permute-start = (bf16[80,320]{1,0:T(8,128)(2,1)}, bf16[80,320]{1,0:T(8,128)(2,1)S(1)}, u32[]{:S(2)}, u32[]{:S(2)}) collective-permute-start(bf16[80,320]{1,0:T(8,128)(2,1)} %bitcast.78), channel_id=1, source_target_pairs={{0,0},{8,8},{16,128},{24,136},{32,256},{40,264},{48,384},{56,392},... | collective-permute-start | bytes 153608 | tf_op jit(solution)/shard_map/ppermute | solution.py:223
  19.0 3.5 %collective-permute-start.1 = (bf16[192,1024]{1,0:T(8,128)(2,1)S(1)}, bf16[192,1024]{1,0:T(8,128)(2,1)S(1)}, u32[]{:S(2)}, u32[]{:S(2)}) collective-permute-start(bf16[192,1024]{1,0:T(8,128)(2,1)S(1)} %convolution_convert_fusion.2), channel_id=1, source_target_pairs={{0,0},{8,64},{16,128},{24,192},{32,256},{40,320},{48,384},{56,448}... | collective-permute-start | bytes 1179656 | tf_op jit(solution)/shard_map/ppermute | solution.py:253
  22.5 28.3 %all-gather = bf16[1280,320]{1,0:T(8,128)(2,1)S(1)} all-gather(bf16[160,320]{1,0:T(8,128)(2,1)S(1)} %pad_maximum_fusion), channel_id=2, replica_groups=mesh['gx'=4,'gc'=2,'z'=8,'y'=8] {'y'}, dimensions={0}, use_global_device_ids=true | all-gather | bytes 921600 | tf_op jit(solution)/shard_map/all_gather | solution.py:252
  54.3 11.2 %collective-permute-start.2 = (bf16[96,1024]{1,0:T(8,128)(2,1)S(1)}, bf16[96,1024]{1,0:T(8,128)(2,1)S(1)}, u32[]{:S(2)}, u32[]{:S(2)}) collective-permute-start(bf16[96,1024]{1,0:T(8,128)(2,1)S(1)} %get-tuple-element.42.refs_0_), channel_id=1, source_target_pairs={{0,128},{128,256},{256,384},{384,0},{1,129},{129,257},{257,385},{3... | collective-permute-start | bytes 589832 | tf_op jit(solution)/shard_map/ppermute | solution.py:23
  65.4 1.9 collective-permute-start.5
  67.4 3.9 %collective-permute-start.3 = (bf16[96,1024]{1,0:T(8,128)(2,1)S(1)}, bf16[96,1024]{1,0:T(8,128)(2,1)S(1)}, u32[]{:S(2)}, u32[]{:S(2)}) collective-permute-start(bf16[96,1024]{1,0:T(8,128)(2,1)S(1)} %get-tuple-element.41.refs_1_), channel_id=1, source_target_pairs={{0,128},{128,256},{256,384},{384,0},{1,129},{129,257},{257,385},{3... | collective-permute-start | bytes 589832 | tf_op jit(solution)/shard_map/ppermute | solution.py:23
  71.3 1.9 collective-permute-start.4
  73.3 3.9 %collective-permute-start.6 = (bf16[96,1024]{1,0:T(8,128)(2,1)S(1)}, bf16[96,1024]{1,0:T(8,128)(2,1)S(1)}, u32[]{:S(2)}, u32[]{:S(2)}) collective-permute-start(bf16[96,1024]{1,0:T(8,128)(2,1)S(1)} %collective-permute-done.2.refs_2_), channel_id=1, source_target_pairs={{0,128},{128,256},{256,384},{384,0},{1,129},{129,257},{257,385},{3... | collective-permute-start | bytes 589832 | tf_op jit(solution)/shard_map/ppermute | solution.py:23
  79.7 2.2 collective-permute-done.6.refs_6_
  81.9 3.4 %collective-permute-done.7.refs_7_ = bf16[96,1024]{1,0:T(8,128)(2,1)S(1)} collective-permute-done((bf16[96,1024]{1,0:T(8,128)(2,1)}, bf16[96,1024]{1,0:T(8,128)(2,1)S(1)}, u32[]{:S(2)}, u32[]{:S(2)}) %collective-permute-start.7) | collective-permute-done | bytes 196640 | tf_op jit(solution)/shard_map/ppermute | solution.py:23
  85.2 3.9 %shard_map.130 = bf16[64,64,128]{2,1,0:T(8,128)(2,1)S(1)} custom-call(s32[4]{0:T(128)S(1)} %pad_add_fusion.order, bf16[96,1024]{1,0:T(8,128)(2,1)S(1)} %get-tuple-element.42.refs_0_, bf16[96,1024]{1,0:T(8,128)(2,1)S(1)} %get-tuple-element.41.refs_1_, bf16[96,1024]{1,0:T(8,128)(2,1)S(1)} %collective-permute-done.2.refs_2_, ...), custom_call_target="tpu_custom_call" | custom-call | tf_op jit(solution)/shard_map/pallas_call | solution.py:66
  90.1 10.1 %all-to-all-start = ((bf16[64,64,128]{2,1,0:T(8,128)(2,1)}), bf16[64,64,128]{2,1,0:T(8,128)(2,1)}, u32[]{:S(2)}, u32[]{:S(2)}) async-start(bf16[64,64,128]{2,1,0:T(8,128)(2,1)} %copy-done.1), calls=%async_computation | async-start | bytes 2097152 | tf_op jit(solution)/shard_map/all_to_all | solution.py:271
  104.8 28.9 %all-to-all-done.arrived = bf16[64,64,128]{2,1,0:T(8,128)(2,1)} async-done(((bf16[64,64,128]{2,1,0:T(8,128)(2,1)}), bf16[64,64,128]{2,1,0:T(8,128)(2,1)}, u32[]{:S(2)}, u32[]{:S(2)}) %all-to-all-start) | async-done | bytes 1048608 | tf_op jit(solution)/shard_map/all_to_all | solution.py:271
  138.6 13.8 %all_gather.21.grads = bf16[4,192,320]{2,1,0:T(8,128)(2,1)S(1)} all-gather(bf16[1,192,320]{2,1,0:T(8,128)(2,1)S(1)} %fusion.19), channel_id=1, replica_groups=mesh['gx'=4,'gc'=2,'z'=8,'y'=8] {'gx'}, dimensions={0}, use_global_device_ids=true | all-gather | bytes 614400 | tf_op jit(solution)/shard_map/all_gather | solution.py:283
  152.4 2.2 copy-done.2
  159.7 15.3 %all_gather.23.near = bf16[384,1280]{1,0:T(8,128)(2,1)S(1)} all-gather(bf16[96,1280]{1,0:T(8,128)(2,1)S(1)} %shard_map.133), channel_id=1, replica_groups=mesh['gx'=4,'gc'=2,'z'=8,'y'=8] {'gx'}, dimensions={0}, use_global_device_ids=true | all-gather | bytes 1228800 | tf_op jit(solution)/shard_map/all_gather | solution.py:315
  175.1 2.1 collective-permute-start.11
  179.6 2.9 %shard_map.134 = bf16[64,56,128]{2,1,0:T(8,128)(2,1)S(1)} custom-call(bf16[384,1280]{1,0:T(8,128)(2,1)S(1)} %all_gather.23.near, bf16[384,1280]{1,0:T(8,128)(2,1)} %collective-permute-done.11.far, bf16[768,320]{1,0:T(8,128)(2,1)S(1)} %get-tuple-element.49.activation), custom_call_target="tpu_custom_call" | custom-call | tf_op jit(solution)/shard_map/pallas_call | solution.py:173
  183.5 7.5 %all-to-all-start.1 = ((bf16[64,56,128]{2,1,0:T(8,128)(2,1)}), bf16[64,56,128]{2,1,0:T(8,128)(2,1)}, u32[]{:S(2)}, u32[]{:S(2)}) async-start(bf16[64,56,128]{2,1,0:T(8,128)(2,1)} %copy-done.3), calls=%async_computation.1 | async-start | bytes 1835008 | tf_op jit(solution)/shard_map/all_to_all | solution.py:319
  191.0 2.5 %slice.35 = bf16[64,20,320]{2,1,0:T(8,128)(2,1)} slice(bf16[64,32,320]{2,1,0:T(8,128)(2,1)} %bitcast.70), slice={[0:64], [0:20], [0:320]} | slice | bytes 1638400 | tf_op jit(solution)/shard_map/slice | solution.py:323
  193.5 2.3 %reshape.486 = bf16[1280,320]{1,0:T(8,128)(2,1)} reshape(bf16[64,20,320]{2,1,0:T(8,128)(2,1)} %slice.35) | data formatting | bytes 1638400 | tf_op jit(solution)/shard_map/reshape | solution.py:323
  199.6 4.7 %fusion.6 = bf16[768,1,320]{0,2,1:T(8,128)(2,1)} fusion(s32[768]{0:T(1024)S(1)} %constant_dynamic-update-slice_fusion.3, bf16[768,1280]{1,0:T(8,128)(2,1)} %copy-done.4, bf16[1280,320]{1,0:T(8,128)(2,1)S(1)} %copy-done.5, f32[768,320]{1,0:T(8,128)} %get-tuple-element.50), kind=kOutput, calls=%fused_computation.11 | convolution fusion | flops 1009926144 | bytes 4262912 | tf_op jit(solution)/shard_map/dot_general | solution.py:326
  204.2 13.7 %all-to-all-done.1.arrived = bf16[64,56,128]{2,1,0:T(8,128)(2,1)} async-done(((bf16[64,56,128]{2,1,0:T(8,128)(2,1)}), bf16[64,56,128]{2,1,0:T(8,128)(2,1)}, u32[]{:S(2)}, u32[]{:S(2)}) %all-to-all-start.1) | async-done | bytes 917536 | tf_op jit(solution)/shard_map/all_to_all | solution.py:319
  217.9 2.0 shard_map.135
  (123 shorter events, 34.1 us)
Async XLA Ops:
  7.2 150.7 %copy-start = (bf16[768,1,1280]{2,0,1:T(8,128)(2,1)S(1)}, bf16[768,1,1280]{2,0,1:T(8,128)(2,1)}, u32[]{:S(2)}) copy-start(bf16[768,1,1280]{2,0,1:T(8,128)(2,1)} %param.16) | copy-start | bytes 5898244
  7.2 11.6 %copy-start.7 = (bf16[128,320]{0,1:T(8,128)(2,1)S(1)}, bf16[128,320]{0,1:T(8,128)(2,1)}, u32[]{:S(2)}) copy-start(bf16[128,320]{0,1:T(8,128)(2,1)} %param.19) | copy-start | bytes 245764
  7.2 145.2 %all-gather.4.cloned.1.call-start = ((), (), s32[]{:S(2)}) async-start(), calls=%async_computation.2 | async-start | bytes 3993600 | tf_op jit(solution)/shard_map/all_gather | solution.py:251
  7.2 10.9 %collective-permute-start = (bf16[80,320]{1,0:T(8,128)(2,1)}, bf16[80,320]{1,0:T(8,128)(2,1)S(1)}, u32[]{:S(2)}, u32[]{:S(2)}) collective-permute-start(bf16[80,320]{1,0:T(8,128)(2,1)} %bitcast.78), channel_id=1, source_target_pairs={{0,0},{8,8},{16,128},{24,136},{32,256},{40,264},{48,384},{56,392},... | collective-permute-start | bytes 153608 | tf_op jit(solution)/shard_map/ppermute | solution.py:223
  19.0 33.4 %collective-permute-start.1 = (bf16[192,1024]{1,0:T(8,128)(2,1)S(1)}, bf16[192,1024]{1,0:T(8,128)(2,1)S(1)}, u32[]{:S(2)}, u32[]{:S(2)}) collective-permute-start(bf16[192,1024]{1,0:T(8,128)(2,1)S(1)} %convolution_convert_fusion.2), channel_id=1, source_target_pairs={{0,0},{8,64},{16,128},{24,192},{32,256},{40,320},{48,384},{56,448}... | collective-permute-start | bytes 1179656 | tf_op jit(solution)/shard_map/ppermute | solution.py:253
  52.3 32.9 %collective-permute-start.8 = (bf16[8,160,320]{2,1,0:T(8,128)(2,1)S(1)}, bf16[8,160,320]{2,1,0:T(8,128)(2,1)}, u32[]{:S(2)}, u32[]{:S(2)}) collective-permute-start(bf16[8,160,320]{2,1,0:T(8,128)(2,1)S(1)} %bitcast.66), channel_id=1, source_target_pairs={{0,64},{64,0},{1,65},{65,1},{2,66},{66,2},{3,67},{67,3},{4,68},{68... | collective-permute-start | bytes 2457608 | tf_op jit(solution)/shard_map/ppermute | solution.py:23
  54.3 19.0 %collective-permute-start.2 = (bf16[96,1024]{1,0:T(8,128)(2,1)S(1)}, bf16[96,1024]{1,0:T(8,128)(2,1)S(1)}, u32[]{:S(2)}, u32[]{:S(2)}) collective-permute-start(bf16[96,1024]{1,0:T(8,128)(2,1)S(1)} %get-tuple-element.42.refs_0_), channel_id=1, source_target_pairs={{0,128},{128,256},{256,384},{384,0},{1,129},{129,257},{257,385},{3... | collective-permute-start | bytes 589832 | tf_op jit(solution)/shard_map/ppermute | solution.py:23
  65.4 11.8 %collective-permute-start.5 = (bf16[96,1024]{1,0:T(8,128)(2,1)S(1)}, bf16[96,1024]{1,0:T(8,128)(2,1)}, u32[]{:S(2)}, u32[]{:S(2)}) collective-permute-start(bf16[96,1024]{1,0:T(8,128)(2,1)S(1)} %get-tuple-element.41.refs_1_), channel_id=1, source_target_pairs={{0,384},{128,0},{256,128},{384,256},{1,385},{129,1},{257,129},{385... | collective-permute-start | bytes 589832 | tf_op jit(solution)/shard_map/ppermute | solution.py:23
  67.4 11.8 %collective-permute-start.3 = (bf16[96,1024]{1,0:T(8,128)(2,1)S(1)}, bf16[96,1024]{1,0:T(8,128)(2,1)S(1)}, u32[]{:S(2)}, u32[]{:S(2)}) collective-permute-start(bf16[96,1024]{1,0:T(8,128)(2,1)S(1)} %get-tuple-element.41.refs_1_), channel_id=1, source_target_pairs={{0,128},{128,256},{256,384},{384,0},{1,129},{129,257},{257,385},{3... | collective-permute-start | bytes 589832 | tf_op jit(solution)/shard_map/ppermute | solution.py:23
  71.3 8.4 %collective-permute-start.4 = (bf16[96,1024]{1,0:T(8,128)(2,1)S(1)}, bf16[96,1024]{1,0:T(8,128)(2,1)S(1)}, u32[]{:S(2)}, u32[]{:S(2)}) collective-permute-start(bf16[96,1024]{1,0:T(8,128)(2,1)S(1)} %get-tuple-element.42.refs_0_), channel_id=1, source_target_pairs={{0,384},{128,0},{256,128},{384,256},{1,385},{129,1},{257,129},{385... | collective-permute-start | bytes 589832 | tf_op jit(solution)/shard_map/ppermute | solution.py:23
  73.3 8.6 %collective-permute-start.6 = (bf16[96,1024]{1,0:T(8,128)(2,1)S(1)}, bf16[96,1024]{1,0:T(8,128)(2,1)S(1)}, u32[]{:S(2)}, u32[]{:S(2)}) collective-permute-start(bf16[96,1024]{1,0:T(8,128)(2,1)S(1)} %collective-permute-done.2.refs_2_), channel_id=1, source_target_pairs={{0,128},{128,256},{256,384},{384,0},{1,129},{129,257},{257,385},{3... | collective-permute-start | bytes 589832 | tf_op jit(solution)/shard_map/ppermute | solution.py:23
  77.2 8.0 %collective-permute-start.7 = (bf16[96,1024]{1,0:T(8,128)(2,1)}, bf16[96,1024]{1,0:T(8,128)(2,1)S(1)}, u32[]{:S(2)}, u32[]{:S(2)}) collective-permute-start(bf16[96,1024]{1,0:T(8,128)(2,1)} %collective-permute-done.5.refs_5_), channel_id=1, source_target_pairs={{0,384},{128,0},{256,128},{384,256},{1,385},{129,1},{257,129},{385... | collective-permute-start | bytes 589832 | tf_op jit(solution)/shard_map/ppermute | solution.py:23
  90.1 10.7 %copy-start.11 = (f32[1280]{0:T(1024)S(1)}, f32[1280]{0:T(1024)}, u32[]{:S(2)}) copy-start(f32[1280]{0:T(1024)} %param.18) | copy-start | bytes 15364
  90.1 11.4 %copy-start.6 = (bf16[192,1,320]{2,0,1:T(8,128)(2,1)S(1)}, bf16[192,1,320]{2,0,1:T(8,128)(2,1)}, u32[]{:S(2)}) copy-start(bf16[192,1,320]{2,0,1:T(8,128)(2,1)} %param.15) | copy-start | bytes 368644
  90.1 43.6 %all-to-all-start = ((bf16[64,64,128]{2,1,0:T(8,128)(2,1)}), bf16[64,64,128]{2,1,0:T(8,128)(2,1)}, u32[]{:S(2)}, u32[]{:S(2)}) async-start(bf16[64,64,128]{2,1,0:T(8,128)(2,1)} %copy-done.1), calls=%async_computation | async-start | bytes 2097152 | tf_op jit(solution)/shard_map/all_to_all | solution.py:271
  100.2 1.5 copy-start.10
  100.3 1.6 copy-start.9
  100.3 90.7 %all-gather.6.cloned.1.call-start = ((), (), s32[]{:S(2)}) async-start(), calls=%async_computation.3 | async-start | bytes 1769472 | tf_op jit(solution)/shard_map/all_gather | solution.py:279
  135.3 3.2 %collective-permute-start.9 = (bf16[96,320]{1,0:T(8,128)(2,1)S(1)}, bf16[96,320]{1,0:T(8,128)(2,1)S(1)}, u32[]{:S(2)}, u32[]{:S(2)}) collective-permute-start(bf16[96,320]{1,0:T(8,128)(2,1)S(1)} %get-tuple-element.30), channel_id=1, source_target_pairs={{0,64},{64,0},{1,65},{65,1},{2,66},{66,2},{3,67},{67,3},{4,68},{68... | collective-permute-start | bytes 184328 | tf_op jit(solution)/shard_map/ppermute | solution.py:23
  152.4 2.2 copy-start.2
  156.0 3.4 %collective-permute-start.10 = (bf16[96,1280]{1,0:T(8,128)(2,1)S(1)}, bf16[96,1280]{1,0:T(8,128)(2,1)S(1)}, u32[]{:S(2)}, u32[]{:S(2)}) collective-permute-start(bf16[96,1280]{1,0:T(8,128)(2,1)S(1)} %get-tuple-element.33), channel_id=1, source_target_pairs={{0,64},{64,0},{1,65},{65,1},{2,66},{66,2},{3,67},{67,3},{4,68},{68... | collective-permute-start | bytes 737288 | tf_op jit(solution)/shard_map/ppermute | solution.py:23
  159.4 18.0 %copy-start.12 = (bf16[768,1,320]{0,2,1:T(8,128)(2,1)S(1)}, bf16[768,1,320]{0,2,1:T(8,128)(2,1)}, u32[]{:S(2)}) copy-start(bf16[768,1,320]{0,2,1:T(8,128)(2,1)} %param.17) | copy-start | bytes 1474564
  175.1 4.6 %collective-permute-start.11 = (bf16[384,1280]{1,0:T(8,128)(2,1)S(1)}, bf16[384,1280]{1,0:T(8,128)(2,1)}, u32[]{:S(2)}, u32[]{:S(2)}) collective-permute-start(bf16[384,1280]{1,0:T(8,128)(2,1)S(1)} %all_gather.23.near), channel_id=1, source_target_pairs={{0,64},{64,0},{1,65},{65,1},{2,66},{66,2},{3,67},{67,3},{4,68},{68... | collective-permute-start | bytes 2949128 | tf_op jit(solution)/shard_map/ppermute | solution.py:23
  183.5 34.4 %all-to-all-start.1 = ((bf16[64,56,128]{2,1,0:T(8,128)(2,1)}), bf16[64,56,128]{2,1,0:T(8,128)(2,1)}, u32[]{:S(2)}, u32[]{:S(2)}) async-start(bf16[64,56,128]{2,1,0:T(8,128)(2,1)} %copy-done.3), calls=%async_computation.1 | async-start | bytes 1835008 | tf_op jit(solution)/shard_map/all_to_all | solution.py:319
  (5 other events, 5.1 us)
Sparse Core Ops, SparseCore 0:
  18.9 107.4 all-gather.3
  137.4 38.8 all-gather.5

commit v5 on v4

--- a/solution.py
+++ b/solution.py
@@ -246,10 +246,9 @@
     pick = (wanted[:, None] == jnp.arange(llm_grad.shape[0], dtype=jnp.int32)[None, :]).astype(BF16)
     rows = jnp.dot(pick, llm_grad, preferred_element_type=F32).astype(BF16)
 
-    fc2_rows = jnp.pad(vit_fc2_w, ((0, 12), (0, 0)))
-    rows, fc2_rows, in_w = lax.optimization_barrier((rows, fc2_rows, in_w))
+    rows, vit_fc2_w, in_w = lax.optimization_barrier((rows, vit_fc2_w, in_w))
     table = lax.all_gather(in_w, SEQ, axis=0, tiled=True)
-    along_y = lax.all_gather(jnp.concatenate([merger_out_w, fc2_rows], axis=0), "y", axis=0)
+    along_y = lax.all_gather(jnp.pad(jnp.concatenate([merger_out_w, vit_fc2_w], axis=0), ((0, 12), (0, 0))), "y", axis=0)
     turned = lax.ppermute(
         rows, (*GRP, "z"), [(g * 8 + z, z * 8 + g) for g in range(8) for z in range(8)]
     )

time: 228 us -> 229 us (level)
  no operation moved by 1% of the time
where the time goes in v5:
time: 229 us; the launch traced here: 228 us
  starting transfers between devices  61.6 us (27%)
  blocking collectives  57.7 us (25%)
  waiting for transfers between devices  51.5 us (22%)
  local copies, waits for them, and re-layouts  19.6 us (9%)
  between operations  14.6 us (6%)
  Pallas kernels  12.1 us (5%)
  matrix products  9.58 us (4%)
    ppermute x10, starting transfers between devices, shifted(): lax.ppermute(value, axis, [(i, (i + step) % size) for i in range(size)])  33.6 us
    all_to_all x1, waiting for transfers between devices, on_device(): lax.all_to_all(partial, SEQ, split_axis=0, concat_axis=0, tiled=True)  28.6 us
    all_gather x1, blocking collectives, on_device(): lax.all_gather(jnp.pad(jnp.concatenate([merger_out_w, vit_fc2_w], axis=0)...  28.3 us
    all_gather x1, blocking collectives, on_device(): near_grad = lax.all_gather(grad, 'gx', axis=0, tiled=True)  15.3 us
    all_gather x1, blocking collectives, on_device(): own, other = merged_products(lax.all_gather(pre_grad, 'gx', axis=0), table)  14.1 us
    all_to_all x1, waiting for transfers between devices, on_device(): lax.all_to_all(sent, SEQ, split_axis=0, concat_axis=0, tiled=True)  13.7 us
    all_to_all x1, starting transfers between devices, on_device(): lax.all_to_all(partial, SEQ, split_axis=0, concat_axis=0, tiled=True)  10.2 us
    ppermute x10, waiting for transfers between devices, shifted(): lax.ppermute(value, axis, [(i, (i + step) % size) for i in range(size)])  8.45 us
  transfers between devices with their start and end apart: 16, of which 9 were waited for; matrix products, arithmetic and copies ran while one was open for 11% of the time, Pallas kernels for 4%

profile of v5, /device:TPU:2, one launch (start us, length us, event | category | flops | bytes accessed | tf_op | source)
XLA Modules:
  0.0 227.7 jit_solution(17218801518318294378)
XLA Ops:
  7.2 6.2 %collective-permute-start = (bf16[80,320]{1,0:T(8,128)(2,1)}, bf16[80,320]{1,0:T(8,128)(2,1)S(1)}, u32[]{:S(2)}, u32[]{:S(2)}) collective-permute-start(bf16[80,320]{1,0:T(8,128)(2,1)} %bitcast.78), channel_id=1, source_target_pairs={{0,0},{8,8},{16,128},{24,136},{32,256},{40,264},{48,384},{56,392},... | collective-permute-start | bytes 153608 | tf_op jit(solution)/shard_map/ppermute | solution.py:223
  19.1 4.2 %collective-permute-start.1 = (bf16[192,1024]{1,0:T(8,128)(2,1)S(1)}, bf16[192,1024]{1,0:T(8,128)(2,1)S(1)}, u32[]{:S(2)}, u32[]{:S(2)}) collective-permute-start(bf16[192,1024]{1,0:T(8,128)(2,1)S(1)} %convolution_convert_fusion.2), channel_id=1, source_target_pairs={{0,0},{8,64},{16,128},{24,192},{32,256},{40,320},{48,384},{56,448}... | collective-permute-start | bytes 1179656 | tf_op jit(solution)/shard_map/ppermute | solution.py:252
  23.4 28.3 %all-gather = bf16[1280,320]{1,0:T(8,128)(2,1)S(1)} all-gather(bf16[160,320]{1,0:T(8,128)(2,1)S(1)} %fusion.26), channel_id=2, replica_groups=mesh['gx'=4,'gc'=2,'z'=8,'y'=8] {'y'}, dimensions={0}, use_global_device_ids=true | all-gather | bytes 921600 | tf_op jit(solution)/shard_map/all_gather | solution.py:251
  54.2 12.0 %collective-permute-start.2 = (bf16[96,1024]{1,0:T(8,128)(2,1)S(1)}, bf16[96,1024]{1,0:T(8,128)(2,1)S(1)}, u32[]{:S(2)}, u32[]{:S(2)}) collective-permute-start(bf16[96,1024]{1,0:T(8,128)(2,1)S(1)} %get-tuple-element.42.refs_0_), channel_id=1, source_target_pairs={{0,128},{128,256},{256,384},{384,0},{1,129},{129,257},{257,385},{3... | collective-permute-start | bytes 589832 | tf_op jit(solution)/shard_map/ppermute | solution.py:23
  66.3 1.9 collective-permute-start.5
  68.2 3.9 %collective-permute-start.3 = (bf16[96,1024]{1,0:T(8,128)(2,1)S(1)}, bf16[96,1024]{1,0:T(8,128)(2,1)S(1)}, u32[]{:S(2)}, u32[]{:S(2)}) collective-permute-start(bf16[96,1024]{1,0:T(8,128)(2,1)S(1)} %get-tuple-element.41.refs_1_), channel_id=1, source_target_pairs={{0,128},{128,256},{256,384},{384,0},{1,129},{129,257},{257,385},{3... | collective-permute-start | bytes 589832 | tf_op jit(solution)/shard_map/ppermute | solution.py:23
  74.1 3.9 %collective-permute-start.6 = (bf16[96,1024]{1,0:T(8,128)(2,1)S(1)}, bf16[96,1024]{1,0:T(8,128)(2,1)S(1)}, u32[]{:S(2)}, u32[]{:S(2)}) collective-permute-start(bf16[96,1024]{1,0:T(8,128)(2,1)S(1)} %collective-permute-done.2.refs_2_), channel_id=1, source_target_pairs={{0,128},{128,256},{256,384},{384,0},{1,129},{129,257},{257,385},{3... | collective-permute-start | bytes 589832 | tf_op jit(solution)/shard_map/ppermute | solution.py:23
  78.0 2.0 collective-permute-start.7
  80.5 2.3 %collective-permute-done.6.refs_6_ = bf16[96,1024]{1,0:T(8,128)(2,1)S(1)} collective-permute-done((bf16[96,1024]{1,0:T(8,128)(2,1)S(1)}, bf16[96,1024]{1,0:T(8,128)(2,1)S(1)}, u32[]{:S(2)}, u32[]{:S(2)}) %collective-permute-start.6) | collective-permute-done | bytes 196640 | tf_op jit(solution)/shard_map/ppermute | solution.py:23
  82.8 3.3 %collective-permute-done.7.refs_7_ = bf16[96,1024]{1,0:T(8,128)(2,1)S(1)} collective-permute-done((bf16[96,1024]{1,0:T(8,128)(2,1)}, bf16[96,1024]{1,0:T(8,128)(2,1)S(1)}, u32[]{:S(2)}, u32[]{:S(2)}) %collective-permute-start.7) | collective-permute-done | bytes 196640 | tf_op jit(solution)/shard_map/ppermute | solution.py:23
  86.1 3.9 %shard_map.130 = bf16[64,64,128]{2,1,0:T(8,128)(2,1)S(1)} custom-call(s32[4]{0:T(128)S(1)} %pad_add_fusion.order, bf16[96,1024]{1,0:T(8,128)(2,1)S(1)} %get-tuple-element.42.refs_0_, bf16[96,1024]{1,0:T(8,128)(2,1)S(1)} %get-tuple-element.41.refs_1_, bf16[96,1024]{1,0:T(8,128)(2,1)S(1)} %collective-permute-done.2.refs_2_, ...), custom_call_target="tpu_custom_call" | custom-call | tf_op jit(solution)/shard_map/pallas_call | solution.py:66
  91.0 10.2 %all-to-all-start = ((bf16[64,64,128]{2,1,0:T(8,128)(2,1)}), bf16[64,64,128]{2,1,0:T(8,128)(2,1)}, u32[]{:S(2)}, u32[]{:S(2)}) async-start(bf16[64,64,128]{2,1,0:T(8,128)(2,1)} %copy-done.1), calls=%async_computation | async-start | bytes 2097152 | tf_op jit(solution)/shard_map/all_to_all | solution.py:270
  105.7 28.6 %all-to-all-done.arrived = bf16[64,64,128]{2,1,0:T(8,128)(2,1)} async-done(((bf16[64,64,128]{2,1,0:T(8,128)(2,1)}), bf16[64,64,128]{2,1,0:T(8,128)(2,1)}, u32[]{:S(2)}, u32[]{:S(2)}) %all-to-all-start) | async-done | bytes 1048608 | tf_op jit(solution)/shard_map/all_to_all | solution.py:270
  139.2 14.1 %all_gather.21.grads = bf16[4,192,320]{2,1,0:T(8,128)(2,1)S(1)} all-gather(bf16[1,192,320]{2,1,0:T(8,128)(2,1)S(1)} %fusion.19), channel_id=1, replica_groups=mesh['gx'=4,'gc'=2,'z'=8,'y'=8] {'gx'}, dimensions={0}, use_global_device_ids=true | all-gather | bytes 614400 | tf_op jit(solution)/shard_map/all_gather | solution.py:282
  153.3 2.2 copy-done.2
  160.7 15.3 %all_gather.23.near = bf16[384,1280]{1,0:T(8,128)(2,1)S(1)} all-gather(bf16[96,1280]{1,0:T(8,128)(2,1)S(1)} %shard_map.133), channel_id=1, replica_groups=mesh['gx'=4,'gc'=2,'z'=8,'y'=8] {'gx'}, dimensions={0}, use_global_device_ids=true | all-gather | bytes 1228800 | tf_op jit(solution)/shard_map/all_gather | solution.py:314
  176.0 2.1 collective-permute-start.11
  180.6 2.9 %shard_map.134 = bf16[64,56,128]{2,1,0:T(8,128)(2,1)S(1)} custom-call(bf16[384,1280]{1,0:T(8,128)(2,1)S(1)} %all_gather.23.near, bf16[384,1280]{1,0:T(8,128)(2,1)} %collective-permute-done.11.far, bf16[768,320]{1,0:T(8,128)(2,1)S(1)} %get-tuple-element.49.activation), custom_call_target="tpu_custom_call" | custom-call | tf_op jit(solution)/shard_map/pallas_call | solution.py:173
  184.4 7.4 %all-to-all-start.1 = ((bf16[64,56,128]{2,1,0:T(8,128)(2,1)}), bf16[64,56,128]{2,1,0:T(8,128)(2,1)}, u32[]{:S(2)}, u32[]{:S(2)}) async-start(bf16[64,56,128]{2,1,0:T(8,128)(2,1)} %copy-done.3), calls=%async_computation.1 | async-start | bytes 1835008 | tf_op jit(solution)/shard_map/all_to_all | solution.py:318
  191.9 2.5 %slice.35 = bf16[64,20,320]{2,1,0:T(8,128)(2,1)} slice(bf16[64,32,320]{2,1,0:T(8,128)(2,1)} %bitcast.70), slice={[0:64], [0:20], [0:320]} | slice | bytes 1638400 | tf_op jit(solution)/shard_map/slice | solution.py:322
  194.4 2.3 reshape.486
  200.5 4.6 %fusion.6 = bf16[768,1,320]{0,2,1:T(8,128)(2,1)} fusion(s32[768]{0:T(1024)S(1)} %constant_dynamic-update-slice_fusion.3, bf16[768,1280]{1,0:T(8,128)(2,1)} %copy-done.4, bf16[1280,320]{1,0:T(8,128)(2,1)S(1)} %copy-done.5, f32[768,320]{1,0:T(8,128)} %get-tuple-element.50), kind=kOutput, calls=%fused_computation.11 | convolution fusion | flops 1009926144 | bytes 4262912 | tf_op jit(solution)/shard_map/dot_general | solution.py:325
  205.2 13.7 %all-to-all-done.1.arrived = bf16[64,56,128]{2,1,0:T(8,128)(2,1)} async-done(((bf16[64,56,128]{2,1,0:T(8,128)(2,1)}), bf16[64,56,128]{2,1,0:T(8,128)(2,1)}, u32[]{:S(2)}, u32[]{:S(2)}) %all-to-all-start.1) | async-done | bytes 917536 | tf_op jit(solution)/shard_map/all_to_all | solution.py:318
  218.9 2.0 shard_map.135
  (122 shorter events, 33.3 us)
Async XLA Ops:
  7.2 151.7 %copy-start = (bf16[768,1,1280]{2,0,1:T(8,128)(2,1)S(1)}, bf16[768,1,1280]{2,0,1:T(8,128)(2,1)}, u32[]{:S(2)}) copy-start(bf16[768,1,1280]{2,0,1:T(8,128)(2,1)} %param.16) | copy-start | bytes 5898244
  7.2 16.1 %copy-start.9 = (bf16[20,320]{1,0:T(8,128)(2,1)S(1)}, bf16[20,320]{1,0:T(8,128)(2,1)}, u32[]{:S(2)}) copy-start(bf16[20,320]{1,0:T(8,128)(2,1)} %param.21) | copy-start | bytes 38404
  7.2 146.1 %all-gather.4.cloned.1.call-start = ((), (), s32[]{:S(2)}) async-start(), calls=%async_computation.2 | async-start | bytes 3993600 | tf_op jit(solution)/shard_map/all_gather | solution.py:250
  7.2 10.2 %collective-permute-start = (bf16[80,320]{1,0:T(8,128)(2,1)}, bf16[80,320]{1,0:T(8,128)(2,1)S(1)}, u32[]{:S(2)}, u32[]{:S(2)}) collective-permute-start(bf16[80,320]{1,0:T(8,128)(2,1)} %bitcast.78), channel_id=1, source_target_pairs={{0,0},{8,8},{16,128},{24,136},{32,256},{40,264},{48,384},{56,392},... | collective-permute-start | bytes 153608 | tf_op jit(solution)/shard_map/ppermute | solution.py:223
  19.1 33.2 %collective-permute-start.1 = (bf16[192,1024]{1,0:T(8,128)(2,1)S(1)}, bf16[192,1024]{1,0:T(8,128)(2,1)S(1)}, u32[]{:S(2)}, u32[]{:S(2)}) collective-permute-start(bf16[192,1024]{1,0:T(8,128)(2,1)S(1)} %convolution_convert_fusion.2), channel_id=1, source_target_pairs={{0,0},{8,64},{16,128},{24,192},{32,256},{40,320},{48,384},{56,448}... | collective-permute-start | bytes 1179656 | tf_op jit(solution)/shard_map/ppermute | solution.py:252
  52.3 33.8 %collective-permute-start.8 = (bf16[8,160,320]{2,1,0:T(8,128)(2,1)S(1)}, bf16[8,160,320]{2,1,0:T(8,128)(2,1)}, u32[]{:S(2)}, u32[]{:S(2)}) collective-permute-start(bf16[8,160,320]{2,1,0:T(8,128)(2,1)S(1)} %bitcast.66), channel_id=1, source_target_pairs={{0,64},{64,0},{1,65},{65,1},{2,66},{66,2},{3,67},{67,3},{4,68},{68... | collective-permute-start | bytes 2457608 | tf_op jit(solution)/shard_map/ppermute | solution.py:23
  54.2 19.9 %collective-permute-start.2 = (bf16[96,1024]{1,0:T(8,128)(2,1)S(1)}, bf16[96,1024]{1,0:T(8,128)(2,1)S(1)}, u32[]{:S(2)}, u32[]{:S(2)}) collective-permute-start(bf16[96,1024]{1,0:T(8,128)(2,1)S(1)} %get-tuple-element.42.refs_0_), channel_id=1, source_target_pairs={{0,128},{128,256},{256,384},{384,0},{1,129},{129,257},{257,385},{3... | collective-permute-start | bytes 589832 | tf_op jit(solution)/shard_map/ppermute | solution.py:23
  66.3 11.8 %collective-permute-start.5 = (bf16[96,1024]{1,0:T(8,128)(2,1)S(1)}, bf16[96,1024]{1,0:T(8,128)(2,1)}, u32[]{:S(2)}, u32[]{:S(2)}) collective-permute-start(bf16[96,1024]{1,0:T(8,128)(2,1)S(1)} %get-tuple-element.41.refs_1_), channel_id=1, source_target_pairs={{0,384},{128,0},{256,128},{384,256},{1,385},{129,1},{257,129},{385... | collective-permute-start | bytes 589832 | tf_op jit(solution)/shard_map/ppermute | solution.py:23
  68.2 11.9 %collective-permute-start.3 = (bf16[96,1024]{1,0:T(8,128)(2,1)S(1)}, bf16[96,1024]{1,0:T(8,128)(2,1)S(1)}, u32[]{:S(2)}, u32[]{:S(2)}) collective-permute-start(bf16[96,1024]{1,0:T(8,128)(2,1)S(1)} %get-tuple-element.41.refs_1_), channel_id=1, source_target_pairs={{0,128},{128,256},{256,384},{384,0},{1,129},{129,257},{257,385},{3... | collective-permute-start | bytes 589832 | tf_op jit(solution)/shard_map/ppermute | solution.py:23
  72.2 8.4 %collective-permute-start.4 = (bf16[96,1024]{1,0:T(8,128)(2,1)S(1)}, bf16[96,1024]{1,0:T(8,128)(2,1)S(1)}, u32[]{:S(2)}, u32[]{:S(2)}) collective-permute-start(bf16[96,1024]{1,0:T(8,128)(2,1)S(1)} %get-tuple-element.42.refs_0_), channel_id=1, source_target_pairs={{0,384},{128,0},{256,128},{384,256},{1,385},{129,1},{257,129},{385... | collective-permute-start | bytes 589832 | tf_op jit(solution)/shard_map/ppermute | solution.py:23
  74.1 8.7 %collective-permute-start.6 = (bf16[96,1024]{1,0:T(8,128)(2,1)S(1)}, bf16[96,1024]{1,0:T(8,128)(2,1)S(1)}, u32[]{:S(2)}, u32[]{:S(2)}) collective-permute-start(bf16[96,1024]{1,0:T(8,128)(2,1)S(1)} %collective-permute-done.2.refs_2_), channel_id=1, source_target_pairs={{0,128},{128,256},{256,384},{384,0},{1,129},{129,257},{257,385},{3... | collective-permute-start | bytes 589832 | tf_op jit(solution)/shard_map/ppermute | solution.py:23
  78.0 8.0 %collective-permute-start.7 = (bf16[96,1024]{1,0:T(8,128)(2,1)}, bf16[96,1024]{1,0:T(8,128)(2,1)S(1)}, u32[]{:S(2)}, u32[]{:S(2)}) collective-permute-start(bf16[96,1024]{1,0:T(8,128)(2,1)} %collective-permute-done.5.refs_5_), channel_id=1, source_target_pairs={{0,384},{128,0},{256,128},{384,256},{1,385},{129,1},{257,129},{385... | collective-permute-start | bytes 589832 | tf_op jit(solution)/shard_map/ppermute | solution.py:23
  90.9 10.7 %copy-start.11 = (f32[1280]{0:T(1024)S(1)}, f32[1280]{0:T(1024)}, u32[]{:S(2)}) copy-start(f32[1280]{0:T(1024)} %param.18) | copy-start | bytes 15364
  91.0 11.5 %copy-start.6 = (bf16[192,1,320]{2,0,1:T(8,128)(2,1)S(1)}, bf16[192,1,320]{2,0,1:T(8,128)(2,1)}, u32[]{:S(2)}) copy-start(bf16[192,1,320]{2,0,1:T(8,128)(2,1)} %param.15) | copy-start | bytes 368644
  91.0 43.4 %all-to-all-start = ((bf16[64,64,128]{2,1,0:T(8,128)(2,1)}), bf16[64,64,128]{2,1,0:T(8,128)(2,1)}, u32[]{:S(2)}, u32[]{:S(2)}) async-start(bf16[64,64,128]{2,1,0:T(8,128)(2,1)} %copy-done.1), calls=%async_computation | async-start | bytes 2097152 | tf_op jit(solution)/shard_map/all_to_all | solution.py:270
  101.1 1.5 copy-start.10
  101.1 1.6 copy-start.8
  101.2 90.8 %all-gather.6.cloned.1.call-start = ((), (), s32[]{:S(2)}) async-start(), calls=%async_computation.3 | async-start | bytes 1769472 | tf_op jit(solution)/shard_map/all_gather | solution.py:278
  135.9 3.2 %collective-permute-start.9 = (bf16[96,320]{1,0:T(8,128)(2,1)S(1)}, bf16[96,320]{1,0:T(8,128)(2,1)S(1)}, u32[]{:S(2)}, u32[]{:S(2)}) collective-permute-start(bf16[96,320]{1,0:T(8,128)(2,1)S(1)} %get-tuple-element.30), channel_id=1, source_target_pairs={{0,64},{64,0},{1,65},{65,1},{2,66},{66,2},{3,67},{67,3},{4,68},{68... | collective-permute-start | bytes 184328 | tf_op jit(solution)/shard_map/ppermute | solution.py:23
  153.3 2.2 copy-start.2
  156.9 3.4 %collective-permute-start.10 = (bf16[96,1280]{1,0:T(8,128)(2,1)S(1)}, bf16[96,1280]{1,0:T(8,128)(2,1)S(1)}, u32[]{:S(2)}, u32[]{:S(2)}) collective-permute-start(bf16[96,1280]{1,0:T(8,128)(2,1)S(1)} %get-tuple-element.33), channel_id=1, source_target_pairs={{0,64},{64,0},{1,65},{65,1},{2,66},{66,2},{3,67},{67,3},{4,68},{68... | collective-permute-start | bytes 737288 | tf_op jit(solution)/shard_map/ppermute | solution.py:23
  160.3 18.0 %copy-start.12 = (bf16[768,1,320]{0,2,1:T(8,128)(2,1)S(1)}, bf16[768,1,320]{0,2,1:T(8,128)(2,1)}, u32[]{:S(2)}) copy-start(bf16[768,1,320]{0,2,1:T(8,128)(2,1)} %param.17) | copy-start | bytes 1474564
  176.0 4.6 %collective-permute-start.11 = (bf16[384,1280]{1,0:T(8,128)(2,1)S(1)}, bf16[384,1280]{1,0:T(8,128)(2,1)}, u32[]{:S(2)}, u32[]{:S(2)}) collective-permute-start(bf16[384,1280]{1,0:T(8,128)(2,1)S(1)} %all_gather.23.near), channel_id=1, source_target_pairs={{0,64},{64,0},{1,65},{65,1},{2,66},{66,2},{3,67},{67,3},{4,68},{68... | collective-permute-start | bytes 2949128 | tf_op jit(solution)/shard_map/ppermute | solution.py:23
  184.4 34.4 %all-to-all-start.1 = ((bf16[64,56,128]{2,1,0:T(8,128)(2,1)}), bf16[64,56,128]{2,1,0:T(8,128)(2,1)}, u32[]{:S(2)}, u32[]{:S(2)}) async-start(bf16[64,56,128]{2,1,0:T(8,128)(2,1)} %copy-done.3), calls=%async_computation.1 | async-start | bytes 1835008 | tf_op jit(solution)/shard_map/all_to_all | solution.py:318
  (5 other events, 5.1 us)
Sparse Core Ops, SparseCore 0:
  18.2 107.8 all-gather.3
  138.0 39.1 all-gather.5
